TPU v7x, 256 devices: a whole 4x4x8 slice. The times are simulated.
256 devices in a mesh: gz: 32 (over x, z), gy: 8 (over y, core).
Axes of the slice: x: 4, y: 4, z: 8, core: 2. Of those that a mesh axis runs over, the one named last changes fastest.
Arguments:
- spectrum: float32 [3, 2, 4, 1024, 4096], P(None, None, None, 'gy', 'gz'), may hold values from -6 to 6
- cells: int32 [2, 524288], P(None, ('gz', 'gy')), may hold values from 0 to 4095, as said below
- offsets: float32 [3, 524288], P(None, ('gz', 'gy')), may hold values from 0 to 1
- counts: int32 [256], P(('gz', 'gy')), may hold values from 1 to 2048, as said below
Outputs:
- coefficients: float32 [3, 4, 1024, 4096], P(None, None, 'gy', 'gz')
- interpolated: float32 [3, 524288], P(None, ('gz', 'gy'))
Inputs may be any that keep to these rules, and one draw needn't show every extreme that they name: The particles of device number b = i * (size of gy) + j, at gz index i and gy index j, occupy slots b * 2048 to b * 2048 + 2047. Their base cells lie from two cells before that device's block to the cell just after its last one: along y from j * 128 - 2 to j * 128 + 128 modulo 1024, along z from i * 128 - 2 to i * 128 + 128 modulo 4096. Empty slots hold such cells too. `counts`: live particles of each device fill its first slots; some device has exactly 2048.
All inputs are finite; a program needn't handle non-finite values.
Results may differ from a plain program's by a relative error of at most 0.000096.
Values sent between devices are 32-bit elements; how exact they have to be, the bound alone decides.
No kernel may reach another device: no remote copies, remote signals or barrier semaphores. Data moves between devices by JAX's collectives and lax.ppermute only.
A program may use at most 64 MiB of HBM per device.

v0:
```python
import math

import jax
import jax.numpy as jnp
from jax import lax
from jax.sharding import PartitionSpec as P


def extended(block, sides, width):
    for axis, dim in sides:
        count = lax.axis_size(axis)
        forward = [(i, i + 1) for i in range(count - 1)]
        forward.append((count - 1, 0))
        backward = [(target, source) for source, target in forward]
        low = lax.ppermute(
            lax.slice_in_dim(block, block.shape[dim] - width, None, axis=dim), axis, forward
        )
        high = lax.ppermute(lax.slice_in_dim(block, 0, width, axis=dim), axis, backward)
        block = jnp.concatenate([low, block, high], axis=dim)
    return block


def angle_table(left, right, modulus):
    product = (
        jnp.arange(left, dtype=jnp.int32)[:, None]
        * jnp.arange(right, dtype=jnp.int32)[None, :]
        % modulus
    )
    angles = product.astype(jnp.float32) * (2.0 * math.pi / modulus)
    return (jnp.cos(angles), jnp.sin(angles))


def inverse_lines(items, length):
    radix_b = 128
    radix_a = length // radix_b
    shaped = items.reshape(items.shape[0], items.shape[1], items.shape[2], radix_a, radix_b)
    real_in = shaped[:, 0]
    imag_in = shaped[:, 1]
    highest = lax.Precision.HIGHEST
    cos_a, sin_a = angle_table(radix_a, radix_a, radix_a)
    first_real = jnp.einsum("nmab,ac->nmcb", real_in, cos_a, precision=highest) - jnp.einsum(
        "nmab,ac->nmcb", imag_in, sin_a, precision=highest
    )
    first_imag = jnp.einsum("nmab,ac->nmcb", real_in, sin_a, precision=highest) + jnp.einsum(
        "nmab,ac->nmcb", imag_in, cos_a, precision=highest
    )
    twist_cos, twist_sin = angle_table(radix_a, radix_b, length)
    middle_real = first_real * twist_cos - first_imag * twist_sin
    middle_imag = first_real * twist_sin + first_imag * twist_cos
    cos_b, sin_b = angle_table(radix_b, radix_b, radix_b)
    final = jnp.einsum("nmcb,bd->nmdc", middle_real, cos_b, precision=highest) - jnp.einsum(
        "nmcb,bd->nmdc", middle_imag, sin_b, precision=highest
    )
    return final.reshape(items.shape[0], items.shape[2], length)


def spline_weights(frac):
    cube = frac * frac * frac
    square = frac * frac
    first = (1.0 - frac) * (1.0 - frac) * (1.0 - frac) / 6.0
    second = (3.0 * cube - 6.0 * square + 4.0) / 6.0
    third = (-3.0 * cube + 3.0 * square + 3.0 * frac + 1.0) / 6.0
    fourth = cube / 6.0
    return [first, second, third, fourth]


def sample_points(flat_field, wide_z, base_index, positions, components, planes):
    weight_x = spline_weights(positions[0])
    weight_y = spline_weights(positions[1])
    weight_z = spline_weights(positions[2])
    total_sum = jnp.zeros((flat_field.shape[0], base_index.shape[0]), jnp.float32)
    for step_y in range(4):
        for step_z in range(4):
            picked = jnp.take(
                flat_field, base_index + (step_y * wide_z + step_z), axis=1, mode="clip"
            )
            total_sum = total_sum + picked * (weight_y[step_y] * weight_z[step_z])[None, :]
    grouped = total_sum.reshape(components, planes, base_index.shape[0])
    values = grouped[:, 0] * weight_x[0]
    for plane in range(1, 4):
        values = values + grouped[:, plane] * weight_x[plane]
    return values


def per_device(spectrum, cells, offsets, counts):
    components, halves, planes, rows_y, rows_z = spectrum.shape
    length_z = rows_z * lax.axis_size("gz")
    length_y = rows_y * lax.axis_size("gy")
    z_start = lax.axis_index("gz") * rows_z
    y_start = lax.axis_index("gy") * rows_y
    z_position = z_start + jnp.arange(rows_z, dtype=jnp.int32)
    symbol = (
        4.0 + 2.0 * jnp.cos(z_position.astype(jnp.float32) * (2.0 * math.pi / length_z))
    ) / 6.0
    scaled = spectrum * (1.0 / (symbol * math.sqrt(length_z)))
    z_lines = scaled.reshape(components, halves, planes * rows_y, rows_z)
    real_lines = inverse_lines(
        lax.all_to_all(z_lines, "gz", split_axis=2, concat_axis=3, tiled=True), length_z
    )
    owned = lax.all_to_all(real_lines, "gz", split_axis=2, concat_axis=1, tiled=True)
    coefficients = owned.reshape(components, planes, rows_y, rows_z)
    widened = extended(coefficients, (("gz", 3), ("gy", 2)), 3)
    wide_z = rows_z + 6
    flat_field = widened.reshape(components * planes, (rows_y + 6) * wide_z)
    near_y = (cells[0] - y_start + 2) % length_y - 2
    near_z = (cells[1] - z_start + 2) % length_z - 2
    base_index = (near_y + 2) * wide_z + (near_z + 2)
    slot_count = cells.shape[1]
    live_count = counts[0]
    values = sample_points(flat_field, wide_z, base_index, offsets, components, planes)
    live_mask = jnp.arange(slot_count, dtype=jnp.int32) < live_count
    interpolated = jnp.where(live_mask[None, :], values, jnp.zeros_like(values))
    return (coefficients, interpolated)


def solution(mesh):
    placed = (
        P(None, None, None, "gy", "gz"),
        P(None, ("gz", "gy")),
        P(None, ("gz", "gy")),
        P(("gz", "gy")),
    )
    return jax.shard_map(
        per_device,
        mesh=mesh,
        in_specs=placed,
        out_specs=(P(None, None, "gy", "gz"), P(None, ("gz", "gy"))),
        check_vma=False,
    )
```

profile of v0, /device:TPU:1, one launch (start us, length us, event | category | flops | bytes accessed | tf_op | source)
XLA Modules:
  0.0 299.9 jit_solution(17782499476344839368)
XLA Ops:
  2.2 2.4 copy.98
  4.6 12.0 %all-to-all-start = ((f32[3,2,512,128]{3,1,0,2:T(2,128)}), f32[3,2,512,128]{3,1,0,2:T(2,128)S(1)}, u32[]{:S(2)}, u32[]{:S(2)}) async-start(f32[3,2,512,128]{3,1,0,2:T(2,128)} %bitcast.4), calls=%async_computation | async-start | bytes 3145728 | tf_op jit(solution)/shard_map/all_to_all | solution.py:98
  17.1 36.4 %all-to-all-done = f32[3,2,512,128]{3,1,0,2:T(2,128)S(1)} async-done(((f32[3,2,512,128]{3,1,0,2:T(2,128)}), f32[3,2,512,128]{3,1,0,2:T(2,128)S(1)}, u32[]{:S(2)}, u32[]{:S(2)}) %all-to-all-start) | async-done | bytes 1572896 | tf_op jit(solution)/shard_map/all_to_all | solution.py:98
  59.9 7.6 %copy.150 = f32[3,16,128,32]{1,0,3,2:T(4,128)} copy(f32[3,16,128,32]{2,3,1,0:T(8,128)S(1)} %fusion) | data formatting | bytes 1572864 | tf_op jit(solution)/shard_map/reshape | solution.py:54
  67.6 9.1 %reshape.576 = f32[32,1,6144]{2,1,0:T(1,128)} reshape(f32[4096,3,16]{2,1,0:T(4,128)} %bitcast.141) | data formatting | bytes 1572864
  76.7 7.8 %all-to-all-start.1 = ((f32[32,1,6144]{2,1,0:T(1,128)}), f32[32,1,6144]{2,1,0:T(1,128)S(1)}, u32[]{:S(2)}, u32[]{:S(2)}) async-start(f32[32,1,6144]{2,1,0:T(1,128)} %reshape.576), calls=%async_computation.1 | async-start | bytes 1572864 | tf_op jit(solution)/shard_map/all_to_all | solution.py:100
  84.8 19.3 %all-to-all-done.1 = f32[32,1,6144]{2,1,0:T(1,128)S(1)} async-done(((f32[32,1,6144]{2,1,0:T(1,128)}), f32[32,1,6144]{2,1,0:T(1,128)S(1)}, u32[]{:S(2)}, u32[]{:S(2)}) %all-to-all-start.1) | async-done | bytes 786464 | tf_op jit(solution)/shard_map/all_to_all | solution.py:100
  104.6 2.5 reduce
  107.1 7.1 %reshape.577 = f32[4096,3,16]{2,1,0:T(4,128)} reshape(f32[32,6144]{1,0:T(8,128)S(1)} %reduce) | data formatting | bytes 1572864
  114.2 6.4 %copy.152 = f32[3,16,32,128]{3,1,2,0:T(8,128)S(1)} copy(f32[3,16,32,128]{1,0,3,2:T(4,128)} %bitcast.142) | data formatting | bytes 1572864 | tf_op jit(solution)/shard_map/all_to_all | solution.py:100
  121.2 3.3 %collective-permute-start.1 = (f32[3,4,128,3]{2,1,3,0:T(4,128)S(1)}, f32[3,4,128,3]{2,1,3,0:T(4,128)S(1)}, u32[]{:S(2)}, u32[]{:S(2)}) collective-permute-start(f32[3,4,128,3]{2,1,3,0:T(4,128)S(1)} %copy.106), channel_id=1, source_target_pairs={{8,0},{16,8},{24,16},{32,24},{40,32},{48,40},{56,48},{64,56},{72,6... | collective-permute-start | bytes 55304 | tf_op jit(solution)/shard_map/ppermute | solution.py:18
  125.8 4.9 %collective-permute-done = f32[3,4,128,3]{2,1,3,0:T(4,128)S(1)} collective-permute-done((f32[3,4,128,3]{2,1,3,0:T(4,128)S(1)}, f32[3,4,128,3]{2,1,3,0:T(4,128)S(1)}, u32[]{:S(2)}, u32[]{:S(2)}) %collective-permute-start) | collective-permute-done | bytes 18464 | tf_op jit(solution)/shard_map/ppermute | solution.py:15
  131.2 4.3 %collective-permute-start.3 = (f32[3,4,3,134]{3,2,1,0:T(4,128)S(1)}, f32[3,4,3,134]{3,2,1,0:T(4,128)S(1)}, u32[]{:S(2)}, u32[]{:S(2)}) collective-permute-start(f32[3,4,3,134]{3,2,1,0:T(4,128)S(1)} %get-tuple-element.16), channel_id=1, source_target_pairs={{1,0},{2,1},{3,2},{4,3},{5,4},{6,5},{7,6},{0,7},{9,8},{10,9},{11,1... | collective-permute-start | bytes 57896 | tf_op jit(solution)/shard_map/ppermute | solution.py:18
  138.4 1.9 pad_maximum_fusion
  140.3 2.1 reshape.443
  142.5 5.1 %copy.109 = f32[12,17956]{0,1:T(8,128)} copy(f32[12,17956]{1,0:T(8,128)S(1)} %reshape.443) | data formatting | bytes 1723776 | tf_op jit(solution)/shard_map/reshape | solution.py:104
  147.6 9.1 %gather_fusion.15 = f32[2048,12]{1,0:T(8,128)S(1)} fusion(f32[12,17956]{0,1:T(8,128)} %copy.109, s32[2048]{0:T(1024)S(1)} %broadcast_clamp_fusion), kind=kCustom, calls=%fused_computation.15 | custom fusion | bytes 204800 | tf_op jit(solution)/shard_map/jit(_take)/gather | solution.py:74
  157.1 9.1 %gather_fusion.14 = f32[2048,12]{1,0:T(8,128)S(1)} fusion(f32[12,17956]{0,1:T(8,128)} %copy.109, s32[2048]{0:T(1024)S(1)} %broadcast_clamp_fusion.1), kind=kCustom, calls=%fused_computation.14 | custom fusion | bytes 204800 | tf_op jit(solution)/shard_map/jit(_take)/gather | solution.py:74
  166.5 9.1 %gather_fusion.13 = f32[2048,12]{1,0:T(8,128)S(1)} fusion(f32[12,17956]{0,1:T(8,128)} %copy.109, s32[2048]{0:T(1024)S(1)} %broadcast_clamp_fusion.2), kind=kCustom, calls=%fused_computation.13 | custom fusion | bytes 204800 | tf_op jit(solution)/shard_map/jit(_take)/gather | solution.py:74
  176.0 9.1 %gather_fusion.12 = f32[2048,12]{1,0:T(8,128)S(1)} fusion(f32[12,17956]{0,1:T(8,128)} %copy.109, s32[2048]{0:T(1024)S(1)} %broadcast_clamp_fusion.3), kind=kCustom, calls=%fused_computation.12 | custom fusion | bytes 204800 | tf_op jit(solution)/shard_map/jit(_take)/gather | solution.py:74
  185.4 9.1 %gather_fusion.11 = f32[2048,12]{1,0:T(8,128)S(1)} fusion(f32[12,17956]{0,1:T(8,128)} %copy.109, s32[2048]{0:T(1024)S(1)} %broadcast_clamp_fusion.4), kind=kCustom, calls=%fused_computation.11 | custom fusion | bytes 204800 | tf_op jit(solution)/shard_map/jit(_take)/gather | solution.py:74
  194.9 9.1 %gather_fusion.10 = f32[2048,12]{1,0:T(8,128)S(1)} fusion(f32[12,17956]{0,1:T(8,128)} %copy.109, s32[2048]{0:T(1024)S(1)} %broadcast_clamp_fusion.5), kind=kCustom, calls=%fused_computation.10 | custom fusion | bytes 204800 | tf_op jit(solution)/shard_map/jit(_take)/gather | solution.py:74
  204.3 9.1 %gather_fusion.9 = f32[2048,12]{1,0:T(8,128)S(1)} fusion(f32[12,17956]{0,1:T(8,128)} %copy.109, s32[2048]{0:T(1024)S(1)} %broadcast_clamp_fusion.6), kind=kCustom, calls=%fused_computation.9 | custom fusion | bytes 204800 | tf_op jit(solution)/shard_map/jit(_take)/gather | solution.py:74
  213.8 9.1 %gather_fusion.8 = f32[2048,12]{1,0:T(8,128)S(1)} fusion(f32[12,17956]{0,1:T(8,128)} %copy.109, s32[2048]{0:T(1024)S(1)} %broadcast_clamp_fusion.7), kind=kCustom, calls=%fused_computation.8 | custom fusion | bytes 204800 | tf_op jit(solution)/shard_map/jit(_take)/gather | solution.py:74
  223.2 9.1 %gather_fusion.7 = f32[2048,12]{1,0:T(8,128)S(1)} fusion(f32[12,17956]{0,1:T(8,128)} %copy.109, s32[2048]{0:T(1024)S(1)} %broadcast_clamp_fusion.8), kind=kCustom, calls=%fused_computation.7 | custom fusion | bytes 204800 | tf_op jit(solution)/shard_map/jit(_take)/gather | solution.py:74
  232.7 9.1 %gather_fusion.6 = f32[2048,12]{1,0:T(8,128)S(1)} fusion(f32[12,17956]{0,1:T(8,128)} %copy.109, s32[2048]{0:T(1024)S(1)} %broadcast_clamp_fusion.9), kind=kCustom, calls=%fused_computation.6 | custom fusion | bytes 204800 | tf_op jit(solution)/shard_map/jit(_take)/gather | solution.py:74
  242.1 9.1 %gather_fusion.5 = f32[2048,12]{1,0:T(8,128)S(1)} fusion(f32[12,17956]{0,1:T(8,128)} %copy.109, s32[2048]{0:T(1024)S(1)} %broadcast_clamp_fusion.10), kind=kCustom, calls=%fused_computation.5 | custom fusion | bytes 204800 | tf_op jit(solution)/shard_map/jit(_take)/gather | solution.py:74
  251.6 9.1 %gather_fusion.4 = f32[2048,12]{1,0:T(8,128)S(1)} fusion(f32[12,17956]{0,1:T(8,128)} %copy.109, s32[2048]{0:T(1024)S(1)} %broadcast_clamp_fusion.11), kind=kCustom, calls=%fused_computation.4 | custom fusion | bytes 204800 | tf_op jit(solution)/shard_map/jit(_take)/gather | solution.py:74
  261.0 9.1 %gather_fusion.3 = f32[2048,12]{1,0:T(8,128)S(1)} fusion(f32[12,17956]{0,1:T(8,128)} %copy.109, s32[2048]{0:T(1024)S(1)} %broadcast_clamp_fusion.12), kind=kCustom, calls=%fused_computation.3 | custom fusion | bytes 204800 | tf_op jit(solution)/shard_map/jit(_take)/gather | solution.py:74
  270.5 9.1 %gather_fusion.2 = f32[2048,12]{1,0:T(8,128)S(1)} fusion(f32[12,17956]{0,1:T(8,128)} %copy.109, s32[2048]{0:T(1024)S(1)} %broadcast_clamp_fusion.13), kind=kCustom, calls=%fused_computation.2 | custom fusion | bytes 204800 | tf_op jit(solution)/shard_map/jit(_take)/gather | solution.py:74
  279.9 9.1 %gather_fusion.1 = f32[2048,12]{1,0:T(8,128)S(1)} fusion(f32[12,17956]{0,1:T(8,128)} %copy.109, s32[2048]{0:T(1024)S(1)} %broadcast_clamp_fusion.14), kind=kCustom, calls=%fused_computation.1 | custom fusion | bytes 204800 | tf_op jit(solution)/shard_map/jit(_take)/gather | solution.py:74
  289.4 9.1 %gather_fusion = f32[2048,12]{1,0:T(8,128)S(1)} fusion(f32[12,17956]{0,1:T(8,128)} %copy.109, s32[2048]{0:T(1024)S(1)} %broadcast_clamp_fusion.15), kind=kCustom, calls=%fused_computation | custom fusion | bytes 204800 | tf_op jit(solution)/shard_map/jit(_take)/gather | solution.py:74
  (85 shorter events, 20.5 us)
Async XLA Ops:
  4.6 12.0 %copy-start.2 = (s32[2,2048]{1,0:T(2,128)S(1)}, s32[2,2048]{1,0:T(2,128)}, u32[]{:S(2)}) copy-start(s32[2,2048]{1,0:T(2,128)} %param.5) | copy-start | bytes 49156
  4.6 48.8 %all-to-all-start = ((f32[3,2,512,128]{3,1,0,2:T(2,128)}), f32[3,2,512,128]{3,1,0,2:T(2,128)S(1)}, u32[]{:S(2)}, u32[]{:S(2)}) async-start(f32[3,2,512,128]{3,1,0,2:T(2,128)} %bitcast.4), calls=%async_computation | async-start | bytes 3145728 | tf_op jit(solution)/shard_map/all_to_all | solution.py:98
  67.6 16.9 %copy-start.1 = (f32[3,2048]{1,0:T(4,128)S(1)}, f32[3,2048]{1,0:T(4,128)}, u32[]{:S(2)}) copy-start(f32[3,2048]{1,0:T(4,128)} %param.6) | copy-start | bytes 73732
  76.7 27.4 %all-to-all-start.1 = ((f32[32,1,6144]{2,1,0:T(1,128)}), f32[32,1,6144]{2,1,0:T(1,128)S(1)}, u32[]{:S(2)}, u32[]{:S(2)}) async-start(f32[32,1,6144]{2,1,0:T(1,128)} %reshape.576), calls=%async_computation.1 | async-start | bytes 1572864 | tf_op jit(solution)/shard_map/all_to_all | solution.py:100
  120.6 17.8 %copy-start = (f32[3,16,32,128]{3,1,2,0:T(8,128)}, f32[3,16,32,128]{3,1,2,0:T(8,128)S(1)}, u32[]{:S(2)}) copy-start(f32[3,16,32,128]{3,1,2,0:T(8,128)S(1)} %copy.152) | copy-start | bytes 2359300
  121.2 4.3 %collective-permute-start.1 = (f32[3,4,128,3]{2,1,3,0:T(4,128)S(1)}, f32[3,4,128,3]{2,1,3,0:T(4,128)S(1)}, u32[]{:S(2)}, u32[]{:S(2)}) collective-permute-start(f32[3,4,128,3]{2,1,3,0:T(4,128)S(1)} %copy.106), channel_id=1, source_target_pairs={{8,0},{16,8},{24,16},{32,24},{40,32},{48,40},{56,48},{64,56},{72,6... | collective-permute-start | bytes 55304 | tf_op jit(solution)/shard_map/ppermute | solution.py:18
  124.8 6.0 %collective-permute-start = (f32[3,4,128,3]{2,1,3,0:T(4,128)S(1)}, f32[3,4,128,3]{2,1,3,0:T(4,128)S(1)}, u32[]{:S(2)}, u32[]{:S(2)}) collective-permute-start(f32[3,4,128,3]{2,1,3,0:T(4,128)S(1)} %copy.105), channel_id=1, source_target_pairs={{0,8},{8,16},{16,24},{24,32},{32,40},{40,48},{48,56},{56,64},{64,7... | collective-permute-start | bytes 55304 | tf_op jit(solution)/shard_map/ppermute | solution.py:15
  131.2 7.2 %collective-permute-start.3 = (f32[3,4,3,134]{3,2,1,0:T(4,128)S(1)}, f32[3,4,3,134]{3,2,1,0:T(4,128)S(1)}, u32[]{:S(2)}, u32[]{:S(2)}) collective-permute-start(f32[3,4,3,134]{3,2,1,0:T(4,128)S(1)} %get-tuple-element.16), channel_id=1, source_target_pairs={{1,0},{2,1},{3,2},{4,3},{5,4},{6,5},{7,6},{0,7},{9,8},{10,9},{11,1... | collective-permute-start | bytes 57896 | tf_op jit(solution)/shard_map/ppermute | solution.py:18
  135.5 3.0 collective-permute-start.2
where the time goes:
time: 301 us; the launch traced here: 300 us
  local copies, waits for them, and re-layouts  194 us (64%)
  waiting for transfers between devices  62.4 us (21%)
  starting transfers between devices  28.7 us (10%)
  other arithmetic  7.67 us (3%)
  matrix products  5.53 us (2%)
    gather x48, local copies, waits for them, and re-layouts, sample_points(): jnp.take(flat_field, base_index + (step_y * wide_z + step_z), axis=1, mod...  151 us
    all_to_all x1, waiting for transfers between devices, per_device(): lax.all_to_all(z_lines, 'gz', split_axis=2, concat_axis=3, tiled=True)  36.4 us
    all_to_all x1, waiting for transfers between devices, per_device(): lax.all_to_all(real_lines, 'gz', split_axis=2, concat_axis=1, tiled=True)  19.3 us
    unnamed x8, local copies, waits for them, and re-layouts  16.2 us
    all_to_all x1, starting transfers between devices, per_device(): lax.all_to_all(z_lines, 'gz', split_axis=2, concat_axis=3, tiled=True)  12 us
    all_to_all x1, starting transfers between devices, per_device(): lax.all_to_all(real_lines, 'gz', split_axis=2, concat_axis=1, tiled=True)  7.82 us
    reshape x1, local copies, waits for them, and re-layouts, inverse_lines(): return final.reshape(items.shape[0], items.shape[2], length)  7.64 us
    ppermute x2, starting transfers between devices, extended(): lax.ppermute(lax.slice_in_dim(block, 0, width, axis=dim), axis, backward)  7.6 us
  transfers between devices with their start and end apart: 6, of which 4 were waited for; matrix products, arithmetic and copies ran while one was open for 0% of the time, Pallas kernels for 0%

commit v1 on v0

v1 whole, which is shorter than its diff:
```python
import math

import jax
import jax.numpy as jnp
import numpy as np
from jax import lax
from jax.experimental import pallas as pl
from jax.experimental.pallas import tpu as pltpu
from jax.sharding import PartitionSpec as P

GROUP = 32
CELLS = 128
LINES = 48
SENT = 56
TILE = 256
VMEM = 48 * 1024 * 1024


def split(value):
    high = value.astype(jnp.bfloat16)
    low = (value - high.astype(jnp.float32)).astype(jnp.bfloat16)
    return high, low


def tables():
    length = GROUP * CELLS
    place = np.arange(length, dtype=np.float64).reshape(GROUP, CELLS)
    symbol = (4.0 + 2.0 * np.cos(2.0 * np.pi * place / length)) / 6.0
    scale = 1.0 / (symbol * math.sqrt(length))
    twist = 2.0 * np.pi * np.outer(np.arange(GROUP), np.arange(CELLS)) / length
    columns = np.arange(CELLS)
    outer = 4 * (columns % GROUP) + columns // GROUP
    last = 2.0 * np.pi * (np.outer(np.arange(CELLS), outer) % CELLS) / CELLS
    matrix = np.concatenate([np.cos(last), -np.sin(last)], axis=0).astype(np.float32)
    high = matrix.astype(jnp.bfloat16)
    low = (matrix - high.astype(np.float32)).astype(jnp.bfloat16)
    return (
        np.stack([scale, np.cos(twist), np.sin(twist)]).astype(np.float32),
        np.concatenate([high, low, high], axis=0),
    )


def add(one, two):
    return one[0] + two[0], one[1] + two[1]


def sub(one, two):
    return one[0] - two[0], one[1] - two[1]


def by_i(one):
    return -one[1], one[0]


def turn(one, part, whole):
    part = part % whole
    if part == 0:
        return one
    if 4 * part == whole:
        return by_i(one)
    if 2 * part == whole:
        return -one[0], -one[1]
    if 4 * part == 3 * whole:
        return one[1], -one[0]
    cos = math.cos(2.0 * math.pi * part / whole)
    sin = math.sin(2.0 * math.pi * part / whole)
    if 8 * part == whole:
        return (one[0] - one[1]) * cos, (one[0] + one[1]) * cos
    if 8 * part == 3 * whole:
        return (one[0] + one[1]) * cos, (one[1] - one[0]) * cos
    return one[0] * cos - one[1] * sin, one[0] * sin + one[1] * cos


def dft4(a, b, c, d):
    even, odd = add(a, c), sub(a, c)
    both, diff = add(b, d), by_i(sub(b, d))
    return [add(even, both), add(odd, diff), sub(even, both), sub(odd, diff)]


def dft8(items):
    even = dft4(*items[0::2])
    odd = dft4(*items[1::2])
    odd = [turn(item, place, 8) for place, item in enumerate(odd)]
    return [add(e, o) for e, o in zip(even, odd)] + [sub(e, o) for e, o in zip(even, odd)]


def dft32(items):
    firsts = []
    for j in range(8):
        four = dft4(items[j], items[j + 8], items[j + 16], items[j + 24])
        firsts.append([turn(item, j * r, 32) for r, item in enumerate(four)])
    out = [None] * 32
    for r in range(4):
        for q, item in enumerate(dft8([firsts[j][r] for j in range(8)])):
            out[r + 4 * q] = item
    return out


def lines_kernel(data, table, matrix, out, wide, flat):
    def columns(index, carry):
        base = pl.multiple_of(index // 2 * 32 + index % 2 * 8, 8)
        base_imag = pl.multiple_of(base + 16, 8)
        items = []
        for k1 in range(GROUP):
            scale = table[0, k1 : k1 + 1, :]
            items.append(
                (data[k1, pl.ds(base, 8), :] * scale, data[k1, pl.ds(base_imag, 8), :] * scale)
            )
        pair = []
        for m, item in enumerate(dft32(items)):
            cos, sin = table[1, m : m + 1, :], table[2, m : m + 1, :]
            pair.append((item[0] * cos - item[1] * sin, item[0] * sin + item[1] * cos))
            if m % 2 == 1:
                row = pl.multiple_of(index * 256 + m * 8 - 8, 16)
                real, imag = [jnp.concatenate(parts, axis=0) for parts in zip(*pair)]
                fill(wide, row, 16, real, imag)
                pair = []
        return carry

    lax.fori_loop(0, 6, columns, 0)
    flat[...] = jnp.dot(wide[...], matrix[...], preferred_element_type=jnp.float32)
    lane = lax.broadcasted_iota(jnp.int32, (GROUP, CELLS), 1)
    odd = lane // 32 % 2 == 1
    upper = lane // 64 == 1
    for index in range(6):
        for half in range(2):
            rows = [
                flat[pl.ds(index * 256 + half * 4 + line, GROUP, stride=8), :]
                for line in range(4)
            ]
            turned = jnp.concatenate(rows, axis=0).T
            v = [turned[s * 32 : s * 32 + 32] for s in range(4)]
            w = [
                jnp.where(odd, pltpu.roll(v[1], 32, 1), v[0]),
                jnp.where(odd, v[1], pltpu.roll(v[0], 96, 1)),
                jnp.where(odd, pltpu.roll(v[3], 32, 1), v[2]),
                jnp.where(odd, v[3], pltpu.roll(v[2], 96, 1)),
            ]
            o = [
                jnp.where(upper, pltpu.roll(w[2], 64, 1), w[0]),
                jnp.where(upper, pltpu.roll(w[3], 64, 1), w[1]),
                jnp.where(upper, w[2], pltpu.roll(w[0], 64, 1)),
                jnp.where(upper, w[3], pltpu.roll(w[1], 64, 1)),
            ]
            for line in range(4):
                row = index * 8 + half * 4 + line
                out[pl.ds(row, GROUP, stride=SENT), :] = o[line]
    empty = jnp.zeros((CELLS - LINES, CELLS), jnp.float32)
    for edge in range(6):
        m = 29 + edge if edge < 3 else edge - 3
        rows = [flat[index * 256 + m * 8 : index * 256 + m * 8 + 8, :] for index in range(6)]
        turned = jnp.concatenate(rows + [empty], axis=0).T
        if edge < 3:
            moved = pltpu.roll(turned[96:128], 1, 0)
        else:
            moved = pltpu.roll(turned[0:32], 31, 0)
        out[pl.ds(LINES + edge, GROUP, stride=SENT), :] = moved
    blank = jnp.zeros((GROUP, CELLS), jnp.float32)
    for edge in range(6, 8):
        out[pl.ds(LINES + edge, GROUP, stride=SENT), :] = blank


def transform(received):
    numbers, matrix = tables()
    return pl.pallas_call(
        lines_kernel,
        out_shape=jax.ShapeDtypeStruct((GROUP * SENT, CELLS), jnp.float32),
        scratch_shapes=[
            pltpu.VMEM((GROUP * LINES, 768), jnp.bfloat16),
            pltpu.VMEM((GROUP * LINES, CELLS), jnp.float32),
        ],
        compiler_params=pltpu.CompilerParams(vmem_limit_bytes=VMEM),
        name="lines",
    )(received, jnp.asarray(numbers), jnp.asarray(matrix))


def spline_weights(frac):
    cube = frac * frac * frac
    square = frac * frac
    rest = 1.0 - frac
    return [
        rest * rest * rest / 6.0,
        (3.0 * cube - 6.0 * square + 4.0) / 6.0,
        (-3.0 * cube + 3.0 * square + 3.0 * frac + 1.0) / 6.0,
        cube / 6.0,
    ]


def spread(weights, step):
    out = jnp.where(step == 0, weights[0], 0.0)
    for place in range(1, 4):
        out = jnp.where(step == place, weights[place], out)
    return out


def particle_tile(start, cells, offsets, at, length_y, length_z):
    spot = pl.ds(at, TILE)
    first_y = ((cells[0:1, spot] - start[0] + 2) & (length_y - 1)) - 3
    first_z = ((cells[1:2, spot] - start[1] + 2) & (length_z - 1)) - 3
    weights = [spline_weights(offsets[d : d + 1, spot]) for d in range(3)]
    row = lax.broadcasted_iota(jnp.int32, (CELLS, TILE), 0)
    inner = spread(weights[2], row - first_z)
    edge = lax.broadcasted_iota(jnp.int32, (8, TILE), 0)
    edge = jnp.where(edge < 3, edge - 3, jnp.where(edge < 6, edge + 125, -9999))
    outer = spread(weights[2], edge - first_z)
    full = jnp.concatenate([inner] + [outer] * 16, axis=0)
    return first_y, weights, full


def fill(wide, row, count, inner, outer):
    for at, part in ((0, inner), (CELLS, outer)):
        high, low = split(part)
        wide[pl.ds(row, count), at : at + CELLS] = high
        wide[pl.ds(row, count), at + 256 : at + 256 + CELLS] = high
        wide[pl.ds(row, count), at + 512 : at + 512 + CELLS] = low


def fill_weights(near, full):
    high, low = split(full)
    near[0:256, :] = high
    near[256:512, :] = low
    near[512:768, :] = high


def block_kernel(lengths, start, data, cells, offsets, coefficients, sums, wide, near, held):
    lane = lax.broadcasted_iota(jnp.int32, (LINES, CELLS), 1)
    for group in range(2):
        tails = [data[group * 16 + t, LINES:SENT, :] for t in range(16)]
        turned = jnp.concatenate(tails, axis=0).T[:LINES]
        for t in range(16):
            whole = group * 16 + t
            inner = data[whole, :LINES, :]
            fill(wide, whole * LINES, LINES, inner, jnp.where(lane // 8 == t, turned, 0.0))
            for c in range(3):
                coefficients[c, whole // 8, whole % 8 * 16 : whole % 8 * 16 + 16, :] = inner[
                    c * 16 : c * 16 + 16
                ]

    def tile(index, carry):
        at = pl.multiple_of(index * TILE, TILE)
        first_y, weights, full = particle_tile(start, cells, offsets, at, *lengths)
        fill_weights(near, full)
        held[...] = jnp.dot(wide[...], near[...], preferred_element_type=jnp.float32)
        row = lax.broadcasted_iota(jnp.int32, (8, TILE), 0)
        totals = [[None] * 3 for _ in range(4)]
        for part in range(16):
            side = spread(weights[1], row + (part * 8) - first_y)
            for a in range(4):
                for c in range(3):
                    place = (a * 8 + part // 2) * LINES + c * 16 + part % 2 * 8
                    term = held[place : place + 8, :] * side
                    total = totals[a][c]
                    totals[a][c] = term if total is None else total + term
        for c in range(3):
            total = totals[0][c] * weights[0][0]
            for a in range(1, 4):
                total = total + totals[a][c] * weights[0][a]
            sums[c : c + 1, pl.ds(at, TILE)] = jnp.sum(total, axis=0, keepdims=True)
        return carry

    lax.fori_loop(0, cells.shape[1] // TILE, tile, 0)


def edge_kernel(lengths, start, below, above, cells, offsets, sums, out, wide, near, held):
    lane = lax.broadcasted_iota(jnp.int32, (8, CELLS), 1)
    sides = (below, above)
    tails = [sides[place // 4][place % 4, 24:32, :] for place in range(8)]
    blank = jnp.zeros((64, CELLS), jnp.float32)
    turned = jnp.concatenate(tails + [blank], axis=0).T
    for place in range(8):
        for c in range(3):
            inner = sides[place // 4][place % 4, c * 8 : c * 8 + 8, :]
            first = c * 16 + (8 if place < 4 else 0)
            outer = jnp.where(lane // 8 == place, turned[first : first + 8], 0.0)
            held[(place * 3 + c) * 8 : (place * 3 + c) * 8 + 8, :CELLS] = inner
            held[(place * 3 + c) * 8 : (place * 3 + c) * 8 + 8, CELLS:] = outer
    fill(wide, 0, 192, held[:, :CELLS], held[:, CELLS:])

    def tile(index, carry):
        at = pl.multiple_of(index * TILE, TILE)
        first_y, weights, full = particle_tile(start, cells, offsets, at, *lengths)
        fill_weights(near, full)
        held[...] = jnp.dot(wide[...], near[...], preferred_element_type=jnp.float32)
        row = lax.broadcasted_iota(jnp.int32, (8, TILE), 0)
        low = spread(weights[1], row - 8 - first_y)
        high = spread(weights[1], row + CELLS - first_y)
        slot = at + lax.broadcasted_iota(jnp.int32, (1, TILE), 1)
        for c in range(3):
            total = None
            for a in range(4):
                term = (
                    held[(a * 3 + c) * 8 : (a * 3 + c) * 8 + 8, :] * low
                    + held[((a + 4) * 3 + c) * 8 : ((a + 4) * 3 + c) * 8 + 8, :] * high
                ) * weights[0][a]
                total = term if total is None else total + term
            value = sums[c : c + 1, pl.ds(at, TILE)] + jnp.sum(total, axis=0, keepdims=True)
            out[c : c + 1, pl.ds(at, TILE)] = jnp.where(slot < start[2], value, 0.0)
        return carry

    lax.fori_loop(0, cells.shape[1] // TILE, tile, 0)


def vmem():
    return pl.BlockSpec(memory_space=pltpu.VMEM)


def interpolate_block(lengths, start, data, cells, offsets):
    def body(*refs):
        block_kernel(lengths, *refs)

    slots = cells.shape[1]
    return pl.pallas_call(
        body,
        in_specs=[pl.BlockSpec(memory_space=pltpu.SMEM)] + [vmem()] * 3,
        out_specs=[vmem()] * 2,
        out_shape=[
            jax.ShapeDtypeStruct((3, 4, CELLS, CELLS), jnp.float32),
            jax.ShapeDtypeStruct((3, slots), jnp.float32),
        ],
        scratch_shapes=[
            pltpu.VMEM((GROUP * LINES, 768), jnp.bfloat16),
            pltpu.VMEM((768, TILE), jnp.bfloat16),
            pltpu.VMEM((GROUP * LINES, TILE), jnp.float32),
        ],
        compiler_params=pltpu.CompilerParams(vmem_limit_bytes=VMEM),
        cost_estimate=pl.CostEstimate(
            flops=2 * 1536 * 768 * 2048, bytes_accessed=2_000_000, transcendentals=0
        ),
        name="block",
    )(start, data, cells, offsets)


def interpolate_edges(lengths, start, below, above, cells, offsets, sums):
    def body(*refs):
        edge_kernel(lengths, *refs)

    return pl.pallas_call(
        body,
        in_specs=[pl.BlockSpec(memory_space=pltpu.SMEM)] + [vmem()] * 5,
        out_specs=vmem(),
        out_shape=jax.ShapeDtypeStruct(sums.shape, jnp.float32),
        scratch_shapes=[
            pltpu.VMEM((192, 768), jnp.bfloat16),
            pltpu.VMEM((768, TILE), jnp.bfloat16),
            pltpu.VMEM((192, TILE), jnp.float32),
        ],
        compiler_params=pltpu.CompilerParams(vmem_limit_bytes=VMEM),
        name="edges",
    )(start, below, above, cells, offsets, sums)


def per_device(spectrum, cells, offsets, counts):
    rows_y, rows_z = spectrum.shape[3], spectrum.shape[4]
    count_y, count_z = lax.axis_size("gy"), lax.axis_size("gz")
    lengths = (rows_y * count_y, rows_z * count_z)
    start = jnp.stack(
        [lax.axis_index("gy") * rows_y, lax.axis_index("gz") * rows_z, counts[0]]
    ).astype(jnp.int32)
    by_target = spectrum.reshape(6, GROUP, 16, CELLS).transpose(1, 0, 2, 3)
    received = lax.all_to_all(
        by_target.reshape(GROUP, 96, CELLS), "gz", split_axis=0, concat_axis=0, tiled=True
    )
    lines = transform(received).reshape(GROUP, SENT, CELLS)
    owned = lax.all_to_all(lines, "gz", split_axis=0, concat_axis=0, tiled=True)
    tiles = owned.reshape(4, 8, 7, 8, CELLS)
    top = jnp.stack([tiles[:, 7, i] for i in (1, 3, 5, 6)], axis=1).reshape(4, 32, CELLS)
    bottom = jnp.stack([tiles[:, 0, i] for i in (0, 2, 4, 6)], axis=1).reshape(4, 32, CELLS)
    forward = [(i, (i + 1) % count_y) for i in range(count_y)]
    backward = [(target, source) for source, target in forward]
    below = lax.ppermute(top, "gy", forward)
    above = lax.ppermute(bottom, "gy", backward)
    coefficients, sums = interpolate_block(lengths, start, owned, cells, offsets)
    interpolated = interpolate_edges(lengths, start, below, above, cells, offsets, sums)
    return coefficients, interpolated


def solution(mesh):
    placed = (
        P(None, None, None, "gy", "gz"),
        P(None, ("gz", "gy")),
        P(None, ("gz", "gy")),
        P(("gz", "gy")),
    )
    return jax.shard_map(
        per_device,
        mesh=mesh,
        in_specs=placed,
        out_specs=(P(None, None, "gy", "gz"), P(None, ("gz", "gy"))),
        check_vma=False,
    )
```

time: 301 us -> 103 us (0.34)
  local copies, waits for them, and re-layouts: 194 us -> 1.64 us
  blocking collectives: 0 us -> 48.5 us
  waiting for transfers between devices: 62.4 us -> 21.2 us
  Pallas kernels: 0 us -> 15.3 us
  starting transfers between devices: 28.7 us -> 14.7 us
  other arithmetic: 7.67 us -> 0.09 us
  matrix products: 5.53 us -> 0 us
    gather x48 -> x0, local copies, waits for them, and re-layouts: 151 us -> none  [sample_points(): jnp.take(flat_field, base_index + (step_y * wide_z + step_z), axis=1, mod...]
    all_to_all x0 -> x1, blocking collectives: none -> 48.5 us  [per_device(): lax.all_to_all(by_target.reshape(GROUP, 96, CELLS), 'gz', split_axis=0, c...]
    all_to_all x2 -> x1, waiting for transfers between devices: 55.7 us -> 21.2 us  [per_device(): owned = lax.all_to_all(lines, 'gz', split_axis=0, concat_axis=0, tiled=True)]
    unnamed x8, local copies, waits for them, and re-layouts: 16.2 us -> 0.02 us
    pallas_call x0 -> x3, Pallas kernels: none -> 15.3 us  [the longest x1 7.74 us: interpolate_block(): pl.pallas_call(body, in_specs=[pl.BlockSpec(memory_space=pltpu.SMEM)] + [...]
    reshape x3 -> x1, local copies, waits for them, and re-layouts: 14.9 us -> 1.6 us  [per_device(): by_target = spectrum.reshape(6, GROUP, 16, CELLS).transpose(1, 0, 2, 3)]
    all_to_all x2 -> x1, starting transfers between devices: 19.8 us -> 8.2 us  [per_device(): owned = lax.all_to_all(lines, 'gz', split_axis=0, concat_axis=0, tiled=True)]
    all_to_all x3 -> x0, local copies, waits for them, and re-layouts: 7.83 us -> none  [the longest x2 6.91 us: per_device(): lax.all_to_all(real_lines, 'gz', split_axis=2, concat_axis=1, tiled=True)]
  transfers between devices with their start and end apart: 6 -> 3, of which waited for: 4 -> 1; matrix products, arithmetic and copies ran while one was open for 0% -> 0% of each run, Pallas kernels for 0% -> 8%
where the time goes in v1:
time: 103 us
  blocking collectives  48.5 us (47%)
  waiting for transfers between devices  21.2 us (21%)
  Pallas kernels  15.3 us (15%)
  starting transfers between devices  14.7 us (14%)
  local copies, waits for them, and re-layouts  1.64 us (2%)
  between operations  1.33 us (1%)
    all_to_all x1, blocking collectives, per_device(): lax.all_to_all(by_target.reshape(GROUP, 96, CELLS), 'gz', split_axis=0, c...  48.5 us
    all_to_all x1, waiting for transfers between devices, per_device(): owned = lax.all_to_all(lines, 'gz', split_axis=0, concat_axis=0, tiled=True)  21.2 us
    all_to_all x1, starting transfers between devices, per_device(): owned = lax.all_to_all(lines, 'gz', split_axis=0, concat_axis=0, tiled=True)  8.2 us
    pallas_call x1, Pallas kernels, interpolate_block(): pl.pallas_call(body, in_specs=[pl.BlockSpec(memory_space=pltpu.SMEM)] + [...  7.74 us
    ppermute x1, starting transfers between devices, per_device(): above = lax.ppermute(bottom, 'gy', backward)  5.24 us
    pallas_call x1, Pallas kernels, transform(): pl.pallas_call(lines_kernel, out_shape=jax.ShapeDtypeStruct((GROUP * SENT...  3.83 us
    pallas_call x1, Pallas kernels, interpolate_edges(): pl.pallas_call(body, in_specs=[pl.BlockSpec(memory_space=pltpu.SMEM)] + [...  3.75 us
  transfers between devices with their start and end apart: 3, of which 1 were waited for; matrix products, arithmetic and copies ran while one was open for 0% of the time, Pallas kernels for 8%

profile of v1, /device:TPU:1, one launch (start us, length us, event | category | flops | bytes accessed | tf_op | source)
XLA Modules:
  0.0 102.7 jit_solution(14920559231913214143)
XLA Ops:
  0.6 1.6 %copy.8 = f32[6,32,16,128]{3,2,0,1:T(8,128)S(1)} copy(f32[6,32,16,128]{3,2,1,0:T(8,128)} %bitcast.46) | data formatting | bytes 3145728 | tf_op jit(solution)/shard_map/reshape | solution.py:359
  2.2 0.0 copy-start
  2.3 0.0 copy-start.1
  2.3 48.5 %all_to_all.10.data = f32[32,96,128]{2,1,0:T(8,128)S(1)} all-to-all(f32[32,96,128]{2,1,0:T(8,128)S(1)} %bitcast.45), channel_id=1, replica_groups=mesh['gz'=32,'gy'=8] {'gz'}, dimensions={0} | all-to-all | bytes 3145728 | tf_op jit(solution)/shard_map/all_to_all | solution.py:360
  50.7 0.0 copy-done
  50.7 0.0 copy-done.1
  50.7 3.8 %lines.1 = f32[1792,128]{1,0:T(8,128)} custom-call(f32[32,96,128]{2,1,0:T(8,128)S(1)} %all_to_all.10.data, f32[3,32,128]{2,1,0:T(8,128)S(1)} %copy-done.1, bf16[768,128]{1,0:T(8,128)(2,1)S(1)} %copy-done), custom_call_target="tpu_custom_call" | custom-call | tf_op jit(solution)/shard_map/lines/pallas_call | solution.py:165
  54.6 0.0 copy-start.2
  54.6 0.0 copy-start.3
  54.6 8.2 %all-to-all-start.1 = ((f32[32,56,128]{2,1,0:T(8,128)}), f32[32,56,128]{2,1,0:T(8,128)S(1)}, u32[]{:S(2)}, u32[]{:S(2)}) async-start(f32[32,56,128]{2,1,0:T(8,128)} %bitcast.5), calls=%async_computation.1 | async-start | bytes 1835008 | tf_op jit(solution)/shard_map/all_to_all | solution.py:364
  63.4 0.1 pad_add_fusion.refs_0_
  63.5 21.2 %all-to-all-done.1.refs_1_ = f32[32,56,128]{2,1,0:T(8,128)S(1)} async-done(((f32[32,56,128]{2,1,0:T(8,128)}), f32[32,56,128]{2,1,0:T(8,128)S(1)}, u32[]{:S(2)}, u32[]{:S(2)}) %all-to-all-start.1) | async-done | bytes 917536 | tf_op jit(solution)/shard_map/all_to_all | solution.py:364
  84.7 5.2 %collective-permute-start.1 = (f32[4,32,128]{2,1,0:T(8,128)S(1)}, f32[4,32,128]{2,1,0:T(8,128)S(1)}, u32[]{:S(2)}, u32[]{:S(2)}) collective-permute-start(f32[4,32,128]{2,1,0:T(8,128)S(1)} %maximum_bitcast_fusion.1), channel_id=1, source_target_pairs={{1,0},{2,1},{3,2},{4,3},{5,4},{6,5},{7,6},{0,7},{9,8},{10,9},{11,1... | collective-permute-start | bytes 196616 | tf_op jit(solution)/shard_map/ppermute | solution.py:371
  89.9 1.2 %collective-permute-start = (f32[4,32,128]{2,1,0:T(8,128)S(1)}, f32[4,32,128]{2,1,0:T(8,128)S(1)}, u32[]{:S(2)}, u32[]{:S(2)}) collective-permute-start(f32[4,32,128]{2,1,0:T(8,128)S(1)} %maximum_bitcast_fusion), channel_id=1, source_target_pairs={{0,1},{1,2},{2,3},{3,4},{4,5},{5,6},{6,7},{7,0},{8,9},{9,10},{10,1... | collective-permute-start | bytes 196616 | tf_op jit(solution)/shard_map/ppermute | solution.py:370
  91.1 0.0 copy-done.2
  91.1 0.0 copy-done.3
  91.2 7.7 %block.1 = (f32[3,4,128,128]{3,2,1,0:T(8,128)}, f32[3,2048]{1,0:T(4,128)S(1)}) custom-call(s32[3]{0:T(128)S(1)} %pad_add_fusion.refs_0_, f32[32,56,128]{2,1,0:T(8,128)S(1)} %all-to-all-done.1.refs_1_, s32[2,2048]{1,0:T(2,128)S(1)} %copy-done.3, f32[3,2048]{1,0:T(4,128)S(1)} %copy-done.2), custom_call_target="tpu_custom_call" | custom-call | flops 4831838208 | bytes 2000000 | tf_op jit(solution)/shard_map/block/pallas_call | solution.py:312
  98.9 0.0 collective-permute-done.1.refs_2_
  98.9 0.0 collective-permute-done.refs_1_
  98.9 3.8 %edges.1 = f32[3,2048]{1,0:T(4,128)} custom-call(s32[3]{0:T(128)S(1)} %pad_add_fusion.refs_0_, f32[4,32,128]{2,1,0:T(8,128)S(1)} %collective-permute-done.refs_1_, f32[4,32,128]{2,1,0:T(8,128)S(1)} %collective-permute-done.1.refs_2_, s32[2,2048]{1,0:T(2,128)S(1)} %copy-done.3, f32[3,2048]{1,0:T(4,128)S(1)} %copy-done.2, f32[3,2048]{1,0:T(4,128)S(1)} %get-tuple-element.5.refs_5_), custom_call_target="tpu_custom_call" | custom-call | tf_op jit(solution)/shard_map/edges/pallas_call | solution.py:337
  (3 shorter events, 0.0 us)
Async XLA Ops:
  2.2 48.5 %copy-start = (bf16[768,128]{1,0:T(8,128)(2,1)S(1)}, bf16[768,128]{1,0:T(8,128)(2,1)}, u32[]{:S(2)}) copy-start(bf16[768,128]{1,0:T(8,128)(2,1)} %constant.16.clone.matrix) | copy-start | bytes 589828
  2.3 48.5 %copy-start.1 = (f32[3,32,128]{2,1,0:T(8,128)S(1)}, f32[3,32,128]{2,1,0:T(8,128)}, u32[]{:S(2)}) copy-start(f32[3,32,128]{2,1,0:T(8,128)} %constant.15.clone.table) | copy-start | bytes 147460
  54.6 36.6 %copy-start.2 = (f32[3,2048]{1,0:T(4,128)S(1)}, f32[3,2048]{1,0:T(4,128)}, u32[]{:S(2)}) copy-start(f32[3,2048]{1,0:T(4,128)} %refs_4_.1) | copy-start | bytes 73732
  54.6 36.6 %copy-start.3 = (s32[2,2048]{1,0:T(2,128)S(1)}, s32[2,2048]{1,0:T(2,128)}, u32[]{:S(2)}) copy-start(s32[2,2048]{1,0:T(2,128)} %refs_3_.3) | copy-start | bytes 49156
  54.6 30.1 %all-to-all-start.1 = ((f32[32,56,128]{2,1,0:T(8,128)}), f32[32,56,128]{2,1,0:T(8,128)S(1)}, u32[]{:S(2)}, u32[]{:S(2)}) async-start(f32[32,56,128]{2,1,0:T(8,128)} %bitcast.5), calls=%async_computation.1 | async-start | bytes 1835008 | tf_op jit(solution)/shard_map/all_to_all | solution.py:364
  84.7 14.2 %collective-permute-start.1 = (f32[4,32,128]{2,1,0:T(8,128)S(1)}, f32[4,32,128]{2,1,0:T(8,128)S(1)}, u32[]{:S(2)}, u32[]{:S(2)}) collective-permute-start(f32[4,32,128]{2,1,0:T(8,128)S(1)} %maximum_bitcast_fusion.1), channel_id=1, source_target_pairs={{1,0},{2,1},{3,2},{4,3},{5,4},{6,5},{7,6},{0,7},{9,8},{10,9},{11,1... | collective-permute-start | bytes 196616 | tf_op jit(solution)/shard_map/ppermute | solution.py:371
  89.9 9.0 %collective-permute-start = (f32[4,32,128]{2,1,0:T(8,128)S(1)}, f32[4,32,128]{2,1,0:T(8,128)S(1)}, u32[]{:S(2)}, u32[]{:S(2)}) collective-permute-start(f32[4,32,128]{2,1,0:T(8,128)S(1)} %maximum_bitcast_fusion), channel_id=1, source_target_pairs={{0,1},{1,2},{2,3},{3,4},{4,5},{5,6},{6,7},{7,0},{8,9},{9,10},{10,1... | collective-permute-start | bytes 196616 | tf_op jit(solution)/shard_map/ppermute | solution.py:370

commit v2 on v1

--- a/solution.py
+++ b/solution.py
@@ -13,7 +13,7 @@
 LINES = 48
 SENT = 56
 TILE = 256
-VMEM = 48 * 1024 * 1024
+MIB = 1024 * 1024
 
 
 def split(value):
@@ -113,7 +113,11 @@
             if m % 2 == 1:
                 row = pl.multiple_of(index * 256 + m * 8 - 8, 16)
                 real, imag = [jnp.concatenate(parts, axis=0) for parts in zip(*pair)]
-                fill(wide, row, 16, real, imag)
+                for at, part in ((0, real), (CELLS, imag)):
+                    high, low = split(part)
+                    wide[pl.ds(row, 16), at : at + CELLS] = high
+                    wide[pl.ds(row, 16), at + 256 : at + 256 + CELLS] = high
+                    wide[pl.ds(row, 16), at + 512 : at + 512 + CELLS] = low
                 pair = []
         return carry
 
@@ -169,7 +173,7 @@
             pltpu.VMEM((GROUP * LINES, 768), jnp.bfloat16),
             pltpu.VMEM((GROUP * LINES, CELLS), jnp.float32),
         ],
-        compiler_params=pltpu.CompilerParams(vmem_limit_bytes=VMEM),
+        compiler_params=pltpu.CompilerParams(vmem_limit_bytes=16 * MIB),
         name="lines",
     )(received, jnp.asarray(numbers), jnp.asarray(matrix))
 
@@ -193,169 +197,182 @@
     return out
 
 
-def particle_tile(start, cells, offsets, at, length_y, length_z):
-    spot = pl.ds(at, TILE)
-    first_y = ((cells[0:1, spot] - start[0] + 2) & (length_y - 1)) - 3
-    first_z = ((cells[1:2, spot] - start[1] + 2) & (length_z - 1)) - 3
-    weights = [spline_weights(offsets[d : d + 1, spot]) for d in range(3)]
+def weights_kernel(lengths, cells, offsets, near, side):
+    start_y = lax.axis_index("gy") * CELLS
+    start_z = lax.axis_index("gz") * CELLS
     row = lax.broadcasted_iota(jnp.int32, (CELLS, TILE), 0)
-    inner = spread(weights[2], row - first_z)
+    row_y = lax.broadcasted_iota(jnp.int32, (CELLS + 16, TILE), 0) - 8
     edge = lax.broadcasted_iota(jnp.int32, (8, TILE), 0)
     edge = jnp.where(edge < 3, edge - 3, jnp.where(edge < 6, edge + 125, -9999))
-    outer = spread(weights[2], edge - first_z)
-    full = jnp.concatenate([inner] + [outer] * 16, axis=0)
-    return first_y, weights, full
+    blank = jnp.zeros((8, TILE), jnp.float32)
+
+    def tile(index, carry):
+        spot = pl.ds(pl.multiple_of(index * TILE, TILE), TILE)
+        first_y = ((cells[0:1, spot] - start_y + 2) & (lengths[0] - 1)) - 3
+        first_z = ((cells[1:2, spot] - start_z + 2) & (lengths[1] - 1)) - 3
+        weights = [spline_weights(offsets[d : d + 1, spot]) for d in range(3)]
+        high, low = split(spread(weights[2], row - first_z))
+        near[index, 0:128, :] = high
+        near[index, 128:256, :] = high
+        near[index, 256:384, :] = low
+        outer = spread(weights[2], edge - first_z)
+        coarse = outer.astype(jnp.bfloat16).astype(jnp.float32)
+        block = jnp.concatenate([coarse, outer - coarse, coarse, blank], axis=0)
+        for part in range(4):
+            near[index, 384 + part * 32 : 416 + part * 32, :] = block.astype(jnp.bfloat16)
+        side[index, 0:144, :] = spread(weights[1], row_y - first_y)
+        side[index, 144:152, :] = jnp.concatenate(weights[0] + weights[0], axis=0)
+        return carry
+
+    lax.fori_loop(0, cells.shape[1] // TILE, tile, 0)
 
 
 def fill(wide, row, count, inner, outer):
-    for at, part in ((0, inner), (CELLS, outer)):
-        high, low = split(part)
-        wide[pl.ds(row, count), at : at + CELLS] = high
-        wide[pl.ds(row, count), at + 256 : at + 256 + CELLS] = high
-        wide[pl.ds(row, count), at + 512 : at + 512 + CELLS] = low
-
-
-def fill_weights(near, full):
-    high, low = split(full)
-    near[0:256, :] = high
-    near[256:512, :] = low
-    near[512:768, :] = high
-
-
-def block_kernel(lengths, start, data, cells, offsets, coefficients, sums, wide, near, held):
+    high, low = split(inner)
+    wide[row : row + count, 0:128] = high
+    wide[row : row + count, 128:256] = low
+    wide[row : row + count, 256:384] = high
+    wide[row : row + count, 384:512] = outer.astype(jnp.bfloat16)
+
+
+def turn_tails(tails):
+    rows = []
+    for tail in tails:
+        coarse = tail.astype(jnp.bfloat16).astype(jnp.float32)
+        rows += [coarse, coarse, tail - coarse, jnp.zeros_like(tail)]
+    return jnp.concatenate(rows, axis=0).T
+
+
+def block_kernel(data, near, side, coefficients, sums, wide, held):
     lane = lax.broadcasted_iota(jnp.int32, (LINES, CELLS), 1)
-    for group in range(2):
-        tails = [data[group * 16 + t, LINES:SENT, :] for t in range(16)]
-        turned = jnp.concatenate(tails, axis=0).T[:LINES]
-        for t in range(16):
-            whole = group * 16 + t
+    for group in range(8):
+        turned = turn_tails([data[group * 4 + t, LINES:SENT, :] for t in range(4)])[:LINES]
+        for t in range(4):
+            whole = group * 4 + t
             inner = data[whole, :LINES, :]
-            fill(wide, whole * LINES, LINES, inner, jnp.where(lane // 8 == t, turned, 0.0))
+            fill(wide, whole * LINES, LINES, inner, jnp.where(lane // 32 == t, turned, 0.0))
             for c in range(3):
                 coefficients[c, whole // 8, whole % 8 * 16 : whole % 8 * 16 + 16, :] = inner[
                     c * 16 : c * 16 + 16
                 ]
 
-    def tile(index, carry):
-        at = pl.multiple_of(index * TILE, TILE)
-        first_y, weights, full = particle_tile(start, cells, offsets, at, *lengths)
-        fill_weights(near, full)
-        held[...] = jnp.dot(wide[...], near[...], preferred_element_type=jnp.float32)
-        row = lax.broadcasted_iota(jnp.int32, (8, TILE), 0)
+    def tile(index, slot):
+        held[slot] = jnp.dot(wide[...], near[index], preferred_element_type=jnp.float32)
         totals = [[None] * 3 for _ in range(4)]
         for part in range(16):
-            side = spread(weights[1], row + (part * 8) - first_y)
+            weight = side[index, 8 + part * 8 : 16 + part * 8, :]
             for a in range(4):
                 for c in range(3):
                     place = (a * 8 + part // 2) * LINES + c * 16 + part % 2 * 8
-                    term = held[place : place + 8, :] * side
+                    term = held[slot, place : place + 8, :] * weight
                     total = totals[a][c]
                     totals[a][c] = term if total is None else total + term
         for c in range(3):
-            total = totals[0][c] * weights[0][0]
+            total = totals[0][c] * side[index, 144:145, :]
             for a in range(1, 4):
-                total = total + totals[a][c] * weights[0][a]
-            sums[c : c + 1, pl.ds(at, TILE)] = jnp.sum(total, axis=0, keepdims=True)
-        return carry
-
-    lax.fori_loop(0, cells.shape[1] // TILE, tile, 0)
-
-
-def edge_kernel(lengths, start, below, above, cells, offsets, sums, out, wide, near, held):
-    lane = lax.broadcasted_iota(jnp.int32, (8, CELLS), 1)
+                total = total + totals[a][c] * side[index, 144 + a : 145 + a, :]
+            at = index * TILE
+            sums[c : c + 1, at : at + TILE] = jnp.sum(total, axis=0, keepdims=True)
+
+    for index in range(near.shape[0]):
+        tile(index, index % 2)
+
+
+def edge_kernel(counts, below, above, near, side, sums, out, wide, held):
+    lane = lax.broadcasted_iota(jnp.int32, (16, CELLS), 1)
     sides = (below, above)
-    tails = [sides[place // 4][place % 4, 24:32, :] for place in range(8)]
-    blank = jnp.zeros((64, CELLS), jnp.float32)
-    turned = jnp.concatenate(tails + [blank], axis=0).T
-    for place in range(8):
-        for c in range(3):
-            inner = sides[place // 4][place % 4, c * 8 : c * 8 + 8, :]
-            first = c * 16 + (8 if place < 4 else 0)
-            outer = jnp.where(lane // 8 == place, turned[first : first + 8], 0.0)
-            held[(place * 3 + c) * 8 : (place * 3 + c) * 8 + 8, :CELLS] = inner
-            held[(place * 3 + c) * 8 : (place * 3 + c) * 8 + 8, CELLS:] = outer
-    fill(wide, 0, 192, held[:, :CELLS], held[:, CELLS:])
-
-    def tile(index, carry):
-        at = pl.multiple_of(index * TILE, TILE)
-        first_y, weights, full = particle_tile(start, cells, offsets, at, *lengths)
-        fill_weights(near, full)
-        held[...] = jnp.dot(wide[...], near[...], preferred_element_type=jnp.float32)
-        row = lax.broadcasted_iota(jnp.int32, (8, TILE), 0)
-        low = spread(weights[1], row - 8 - first_y)
-        high = spread(weights[1], row + CELLS - first_y)
+    parts = []
+    for group in range(2):
+        turned = turn_tails([sides[group][a, 24:32, :] for a in range(4)])
+        for a in range(4):
+            for c in range(3):
+                first = c * 16 + (8 if group == 0 else 0)
+                outer = jnp.where(lane[:8] // 32 == a, turned[first : first + 8], 0.0)
+                parts.append((sides[group][a, c * 8 : c * 8 + 8, :], outer))
+    for place in range(0, 24, 2):
+        inner, outer = [jnp.concatenate(pair, axis=0) for pair in zip(*parts[place : place + 2])]
+        fill(wide, place * 8, 16, inner, outer)
+    for index in range(near.shape[0]):
+        at = index * TILE
+        held[index] = jnp.dot(wide[...], near[index], preferred_element_type=jnp.float32)
+        low = side[index, 0:8, :]
+        high = side[index, 136:144, :]
         slot = at + lax.broadcasted_iota(jnp.int32, (1, TILE), 1)
         for c in range(3):
             total = None
             for a in range(4):
                 term = (
-                    held[(a * 3 + c) * 8 : (a * 3 + c) * 8 + 8, :] * low
-                    + held[((a + 4) * 3 + c) * 8 : ((a + 4) * 3 + c) * 8 + 8, :] * high
-                ) * weights[0][a]
+                    held[index, (a * 3 + c) * 8 : (a * 3 + c) * 8 + 8, :] * low
+                    + held[index, ((a + 4) * 3 + c) * 8 : ((a + 4) * 3 + c) * 8 + 8, :] * high
+                ) * side[index, 144 + a : 145 + a, :]
                 total = term if total is None else total + term
-            value = sums[c : c + 1, pl.ds(at, TILE)] + jnp.sum(total, axis=0, keepdims=True)
-            out[c : c + 1, pl.ds(at, TILE)] = jnp.where(slot < start[2], value, 0.0)
-        return carry
-
-    lax.fori_loop(0, cells.shape[1] // TILE, tile, 0)
+            value = sums[c : c + 1, at : at + TILE] + jnp.sum(total, axis=0, keepdims=True)
+            out[c : c + 1, at : at + TILE] = jnp.where(slot < counts[0:1, 0:1], value, 0.0)
 
 
 def vmem():
     return pl.BlockSpec(memory_space=pltpu.VMEM)
 
 
-def interpolate_block(lengths, start, data, cells, offsets):
+def particle_weights(lengths, cells, offsets):
     def body(*refs):
-        block_kernel(lengths, *refs)
-
-    slots = cells.shape[1]
+        weights_kernel(lengths, *refs)
+
+    count = cells.shape[1] // TILE
     return pl.pallas_call(
         body,
-        in_specs=[pl.BlockSpec(memory_space=pltpu.SMEM)] + [vmem()] * 3,
+        in_specs=[vmem()] * 2,
+        out_specs=[vmem()] * 2,
+        out_shape=[
+            jax.ShapeDtypeStruct((count, 512, TILE), jnp.bfloat16),
+            jax.ShapeDtypeStruct((count, CELLS + 24, TILE), jnp.float32),
+        ],
+        compiler_params=pltpu.CompilerParams(vmem_limit_bytes=10 * MIB),
+        cost_estimate=pl.CostEstimate(
+            flops=10_000_000, bytes_accessed=4_000_000, transcendentals=0
+        ),
+        name="weights",
+    )(cells, offsets)
+
+
+def interpolate_block(data, near, side):
+    count = near.shape[0]
+    return pl.pallas_call(
+        block_kernel,
+        in_specs=[vmem()] * 3,
         out_specs=[vmem()] * 2,
         out_shape=[
             jax.ShapeDtypeStruct((3, 4, CELLS, CELLS), jnp.float32),
-            jax.ShapeDtypeStruct((3, slots), jnp.float32),
+            jax.ShapeDtypeStruct((3, count * TILE), jnp.float32),
         ],
         scratch_shapes=[
-            pltpu.VMEM((GROUP * LINES, 768), jnp.bfloat16),
-            pltpu.VMEM((768, TILE), jnp.bfloat16),
-            pltpu.VMEM((GROUP * LINES, TILE), jnp.float32),
+            pltpu.VMEM((GROUP * LINES, 512), jnp.bfloat16),
+            pltpu.VMEM((2, GROUP * LINES, TILE), jnp.float32),
         ],
-        compiler_params=pltpu.CompilerParams(vmem_limit_bytes=VMEM),
-        cost_estimate=pl.CostEstimate(
-            flops=2 * 1536 * 768 * 2048, bytes_accessed=2_000_000, transcendentals=0
-        ),
+        compiler_params=pltpu.CompilerParams(vmem_limit_bytes=16 * MIB),
         name="block",
-    )(start, data, cells, offsets)
-
-
-def interpolate_edges(lengths, start, below, above, cells, offsets, sums):
-    def body(*refs):
-        edge_kernel(lengths, *refs)
-
+    )(data, near, side)
+
+
+def interpolate_edges(counts, below, above, near, side, sums):
     return pl.pallas_call(
-        body,
-        in_specs=[pl.BlockSpec(memory_space=pltpu.SMEM)] + [vmem()] * 5,
+        edge_kernel,
+        in_specs=[vmem()] * 6,
         out_specs=vmem(),
         out_shape=jax.ShapeDtypeStruct(sums.shape, jnp.float32),
         scratch_shapes=[
-            pltpu.VMEM((192, 768), jnp.bfloat16),
-            pltpu.VMEM((768, TILE), jnp.bfloat16),
-            pltpu.VMEM((192, TILE), jnp.float32),
+            pltpu.VMEM((192, 512), jnp.bfloat16),
+            pltpu.VMEM((near.shape[0], 192, TILE), jnp.float32),
         ],
-        compiler_params=pltpu.CompilerParams(vmem_limit_bytes=VMEM),
+        compiler_params=pltpu.CompilerParams(vmem_limit_bytes=10 * MIB),
         name="edges",
-    )(start, below, above, cells, offsets, sums)
+    )(counts, below, above, near, side, sums)
 
 
 def per_device(spectrum, cells, offsets, counts):
     rows_y, rows_z = spectrum.shape[3], spectrum.shape[4]
     count_y, count_z = lax.axis_size("gy"), lax.axis_size("gz")
     lengths = (rows_y * count_y, rows_z * count_z)
-    start = jnp.stack(
-        [lax.axis_index("gy") * rows_y, lax.axis_index("gz") * rows_z, counts[0]]
-    ).astype(jnp.int32)
     by_target = spectrum.reshape(6, GROUP, 16, CELLS).transpose(1, 0, 2, 3)
     received = lax.all_to_all(
         by_target.reshape(GROUP, 96, CELLS), "gz", split_axis=0, concat_axis=0, tiled=True
@@ -367,10 +384,11 @@
     bottom = jnp.stack([tiles[:, 0, i] for i in (0, 2, 4, 6)], axis=1).reshape(4, 32, CELLS)
     forward = [(i, (i + 1) % count_y) for i in range(count_y)]
     backward = [(target, source) for source, target in forward]
+    above = lax.ppermute(bottom, "gy", backward)
     below = lax.ppermute(top, "gy", forward)
-    above = lax.ppermute(bottom, "gy", backward)
-    coefficients, sums = interpolate_block(lengths, start, owned, cells, offsets)
-    interpolated = interpolate_edges(lengths, start, below, above, cells, offsets, sums)
+    near, side = particle_weights(lengths, cells, offsets)
+    coefficients, sums = interpolate_block(owned, near, side)
+    interpolated = interpolate_edges(counts.reshape(1, 1), below, above, near, side, sums)
     return coefficients, interpolated
 
 

time: 103 us -> 96.6 us (0.938)
  blocking collectives: 48.5 us -> 78.2 us
  waiting for transfers between devices: 21.2 us -> 0.01 us
  starting transfers between devices: 14.7 us -> 6.46 us
  Pallas kernels: 15.3 us -> 8.6 us
    all_to_all x0 -> x1, blocking collectives: none -> 29.7 us  [per_device(): owned = lax.all_to_all(lines, 'gz', split_axis=0, concat_axis=0, tiled=True)]
    all_to_all x1 -> x0, waiting for transfers between devices: 21.2 us -> none  [per_device(): owned = lax.all_to_all(lines, 'gz', split_axis=0, concat_axis=0, tiled=True)]
    all_to_all x1 -> x0, starting transfers between devices: 8.2 us -> none  [per_device(): owned = lax.all_to_all(lines, 'gz', split_axis=0, concat_axis=0, tiled=True)]
    pallas_call x2 -> x3, Pallas kernels: 11.5 us -> 5.71 us  [the longest x1 3.47 us: interpolate_block(): pl.pallas_call(block_kernel, in_specs=[vmem()] * 3, out_specs=[vmem()] *...]
  transfers between devices with their start and end apart: 3 -> 2, of which waited for: 1 -> 0; matrix products, arithmetic and copies ran while one was open for 0% -> 0% of each run, Pallas kernels for 8% -> 5%
where the time goes in v2:
time: 96.6 us; the launch traced here: 96.3 us
  blocking collectives  78.2 us (81%)
  Pallas kernels  8.6 us (9%)
  starting transfers between devices  6.46 us (7%)
  local copies, waits for them, and re-layouts  1.64 us (2%)
  between operations  1.38 us (1%)
    all_to_all x1, blocking collectives, per_device(): lax.all_to_all(by_target.reshape(GROUP, 96, CELLS), 'gz', split_axis=0, c...  48.5 us
    all_to_all x1, blocking collectives, per_device(): owned = lax.all_to_all(lines, 'gz', split_axis=0, concat_axis=0, tiled=True)  29.7 us
    ppermute x1, starting transfers between devices, per_device(): above = lax.ppermute(bottom, 'gy', backward)  5.24 us
    pallas_call x1, Pallas kernels, interpolate_block(): pl.pallas_call(block_kernel, in_specs=[vmem()] * 3, out_specs=[vmem()] *...  3.47 us
    pallas_call x1, Pallas kernels, transform(): pl.pallas_call(lines_kernel, out_shape=jax.ShapeDtypeStruct((GROUP * SENT...  2.89 us
  transfers between devices with their start and end apart: 2, of which 0 were waited for; matrix products, arithmetic and copies ran while one was open for 0% of the time, Pallas kernels for 5%

profile of v2, /device:TPU:1, one launch (start us, length us, event | category | flops | bytes accessed | tf_op | source)
XLA Modules:
  0.0 96.3 jit_solution(242869522555033018)
XLA Ops:
  0.6 1.6 %copy.8 = f32[6,32,16,128]{3,2,0,1:T(8,128)S(1)} copy(f32[6,32,16,128]{3,2,1,0:T(8,128)} %bitcast.47) | data formatting | bytes 3145728 | tf_op jit(solution)/shard_map/reshape | solution.py:376
  2.2 0.0 copy-start
  2.3 0.0 copy-start.1
  2.3 48.5 %all_to_all.10.data = f32[32,96,128]{2,1,0:T(8,128)S(1)} all-to-all(f32[32,96,128]{2,1,0:T(8,128)S(1)} %bitcast.46), channel_id=1, replica_groups=mesh['gz'=32,'gy'=8] {'gz'}, dimensions={0} | all-to-all | bytes 3145728 | tf_op jit(solution)/shard_map/all_to_all | solution.py:377
  50.7 0.0 copy-done
  50.7 0.0 copy-done.1
  50.7 2.9 %lines.1 = f32[1792,128]{1,0:T(8,128)S(1)} custom-call(f32[32,96,128]{2,1,0:T(8,128)S(1)} %all_to_all.10.data, f32[3,32,128]{2,1,0:T(8,128)S(1)} %copy-done.1, bf16[768,128]{1,0:T(8,128)(2,1)S(1)} %copy-done), custom_call_target="tpu_custom_call" | custom-call | tf_op jit(solution)/shard_map/lines/pallas_call | solution.py:169
  53.6 0.0 copy-start.2
  53.6 0.0 copy-start.3
  53.6 29.7 %all_to_all.11.data = f32[32,56,128]{2,1,0:T(8,128)S(1)} all-to-all(f32[32,56,128]{2,1,0:T(8,128)S(1)} %bitcast.45), channel_id=1, replica_groups=mesh['gz'=32,'gy'=8] {'gz'}, dimensions={0} | all-to-all | bytes 1835008 | tf_op jit(solution)/shard_map/all_to_all | solution.py:381
  83.4 5.2 %collective-permute-start.1 = (f32[4,32,128]{2,1,0:T(8,128)S(1)}, f32[4,32,128]{2,1,0:T(8,128)S(1)}, u32[]{:S(2)}, u32[]{:S(2)}) collective-permute-start(f32[4,32,128]{2,1,0:T(8,128)S(1)} %maximum_bitcast_fusion.1), channel_id=1, source_target_pairs={{1,0},{2,1},{3,2},{4,3},{5,4},{6,5},{7,6},{0,7},{9,8},{10,9},{11,1... | collective-permute-start | bytes 196616 | tf_op jit(solution)/shard_map/ppermute | solution.py:387
  88.7 1.2 %collective-permute-start = (f32[4,32,128]{2,1,0:T(8,128)S(1)}, f32[4,32,128]{2,1,0:T(8,128)S(1)}, u32[]{:S(2)}, u32[]{:S(2)}) collective-permute-start(f32[4,32,128]{2,1,0:T(8,128)S(1)} %maximum_bitcast_fusion), channel_id=1, source_target_pairs={{0,1},{1,2},{2,3},{3,4},{4,5},{5,6},{6,7},{7,0},{8,9},{9,10},{10,1... | collective-permute-start | bytes 196616 | tf_op jit(solution)/shard_map/ppermute | solution.py:388
  90.5 0.0 copy-done.2
  90.5 0.0 copy-done.3
  90.6 1.0 %weights.1 = (bf16[8,512,256]{2,1,0:T(8,128)(2,1)S(1)}, f32[8,152,256]{2,1,0:T(8,128)S(1)}) custom-call(s32[2,2048]{1,0:T(2,128)S(1)} %copy-done.3, f32[3,2048]{1,0:T(4,128)S(1)} %copy-done.2), custom_call_target="tpu_custom_call" | custom-call | flops 10000000 | bytes 4000000 | tf_op jit(solution)/shard_map/weights/pallas_call | solution.py:322
  91.6 3.5 %block.1 = (f32[3,4,128,128]{3,2,1,0:T(8,128)}, f32[3,2048]{1,0:T(4,128)S(1)}) custom-call(f32[32,56,128]{2,1,0:T(8,128)S(1)} %all_to_all.11.data, bf16[8,512,256]{2,1,0:T(8,128)(2,1)S(1)} %get-tuple-element.6.near, f32[8,152,256]{2,1,0:T(8,128)S(1)} %get-tuple-element.7.side), custom_call_target="tpu_custom_call" | custom-call | tf_op jit(solution)/shard_map/block/pallas_call | solution.py:340
  95.0 0.0 collective-permute-done.1.above
  95.1 0.0 collective-permute-done.below
  95.1 1.2 %edges.1 = f32[3,2048]{1,0:T(4,128)} custom-call(s32[1,1]{1,0:T(1,128)} %bitcast.43.counts, f32[4,32,128]{2,1,0:T(8,128)S(1)} %collective-permute-done.below, f32[4,32,128]{2,1,0:T(8,128)S(1)} %collective-permute-done.1.above, bf16[8,512,256]{2,1,0:T(8,128)(2,1)S(1)} %get-tuple-element.6.near, f32[8,152,256]{2,1,0:T(8,128)S(1)} %get-tuple-element.7.side, ...), custom_call_target="tpu_custom_call" | custom-call | tf_op jit(solution)/shard_map/edges/pallas_call | solution.py:358
  (3 shorter events, 0.0 us)
Async XLA Ops:
  2.2 48.5 %copy-start = (bf16[768,128]{1,0:T(8,128)(2,1)S(1)}, bf16[768,128]{1,0:T(8,128)(2,1)}, u32[]{:S(2)}) copy-start(bf16[768,128]{1,0:T(8,128)(2,1)} %constant.5.clone.matrix) | copy-start | bytes 589828
  2.3 48.5 %copy-start.1 = (f32[3,32,128]{2,1,0:T(8,128)S(1)}, f32[3,32,128]{2,1,0:T(8,128)}, u32[]{:S(2)}) copy-start(f32[3,32,128]{2,1,0:T(8,128)} %constant.4.clone.table) | copy-start | bytes 147460
  53.6 36.9 %copy-start.2 = (f32[3,2048]{1,0:T(4,128)S(1)}, f32[3,2048]{1,0:T(4,128)}, u32[]{:S(2)}) copy-start(f32[3,2048]{1,0:T(4,128)} %refs_1_.1) | copy-start | bytes 73732
  53.6 36.9 %copy-start.3 = (s32[2,2048]{1,0:T(2,128)S(1)}, s32[2,2048]{1,0:T(2,128)}, u32[]{:S(2)}) copy-start(s32[2,2048]{1,0:T(2,128)} %refs_0_.1) | copy-start | bytes 49156
  83.4 11.6 %collective-permute-start.1 = (f32[4,32,128]{2,1,0:T(8,128)S(1)}, f32[4,32,128]{2,1,0:T(8,128)S(1)}, u32[]{:S(2)}, u32[]{:S(2)}) collective-permute-start(f32[4,32,128]{2,1,0:T(8,128)S(1)} %maximum_bitcast_fusion.1), channel_id=1, source_target_pairs={{1,0},{2,1},{3,2},{4,3},{5,4},{6,5},{7,6},{0,7},{9,8},{10,9},{11,1... | collective-permute-start | bytes 196616 | tf_op jit(solution)/shard_map/ppermute | solution.py:387
  88.7 6.4 %collective-permute-start = (f32[4,32,128]{2,1,0:T(8,128)S(1)}, f32[4,32,128]{2,1,0:T(8,128)S(1)}, u32[]{:S(2)}, u32[]{:S(2)}) collective-permute-start(f32[4,32,128]{2,1,0:T(8,128)S(1)} %maximum_bitcast_fusion), channel_id=1, source_target_pairs={{0,1},{1,2},{2,3},{3,4},{4,5},{5,6},{6,7},{7,0},{8,9},{9,10},{10,1... | collective-permute-start | bytes 196616 | tf_op jit(solution)/shard_map/ppermute | solution.py:388

commit v3 on v2

--- a/solution.py
+++ b/solution.py
@@ -11,7 +11,7 @@
 GROUP = 32
 CELLS = 128
 LINES = 48
-SENT = 56
+SENT = 51
 TILE = 256
 MIB = 1024 * 1024
 
@@ -98,8 +98,8 @@
 
 def lines_kernel(data, table, matrix, out, wide, flat):
     def columns(index, carry):
-        base = pl.multiple_of(index // 2 * 32 + index % 2 * 8, 8)
-        base_imag = pl.multiple_of(base + 16, 8)
+        base = index // 2 * 32 + index % 2 * 8
+        base_imag = base + 16
         items = []
         for k1 in range(GROUP):
             scale = table[0, k1 : k1 + 1, :]
@@ -111,7 +111,7 @@
             cos, sin = table[1, m : m + 1, :], table[2, m : m + 1, :]
             pair.append((item[0] * cos - item[1] * sin, item[0] * sin + item[1] * cos))
             if m % 2 == 1:
-                row = pl.multiple_of(index * 256 + m * 8 - 8, 16)
+                row = index * 256 + m * 8 - 8
                 real, imag = [jnp.concatenate(parts, axis=0) for parts in zip(*pair)]
                 for at, part in ((0, real), (CELLS, imag)):
                     high, low = split(part)
@@ -121,7 +121,8 @@
                 pair = []
         return carry
 
-    lax.fori_loop(0, 6, columns, 0)
+    for index in range(6):
+        columns(index, 0)
     flat[...] = jnp.dot(wide[...], matrix[...], preferred_element_type=jnp.float32)
     lane = lax.broadcasted_iota(jnp.int32, (GROUP, CELLS), 1)
     odd = lane // 32 % 2 == 1
@@ -149,19 +150,19 @@
             for line in range(4):
                 row = index * 8 + half * 4 + line
                 out[pl.ds(row, GROUP, stride=SENT), :] = o[line]
-    empty = jnp.zeros((CELLS - LINES, CELLS), jnp.float32)
-    for edge in range(6):
-        m = 29 + edge if edge < 3 else edge - 3
-        rows = [flat[index * 256 + m * 8 : index * 256 + m * 8 + 8, :] for index in range(6)]
-        turned = jnp.concatenate(rows + [empty], axis=0).T
-        if edge < 3:
-            moved = pltpu.roll(turned[96:128], 1, 0)
-        else:
-            moved = pltpu.roll(turned[0:32], 31, 0)
-        out[pl.ds(LINES + edge, GROUP, stride=SENT), :] = moved
-    blank = jnp.zeros((GROUP, CELLS), jnp.float32)
-    for edge in range(6, 8):
-        out[pl.ds(LINES + edge, GROUP, stride=SENT), :] = blank
+    empty = jnp.zeros((16, CELLS), jnp.float32)
+    left = lax.broadcasted_iota(jnp.int32, (GROUP, CELLS), 1) < 64
+    for pair in range(3):
+        rows = []
+        for edge in (2 * pair, 2 * pair + 1):
+            m = 29 + edge if edge < 3 else edge - 3
+            rows += [flat[index * 256 + m * 8 : index * 256 + m * 8 + 8, :] for index in range(6)]
+            rows += [empty]
+        turned = jnp.concatenate(rows, axis=0).T
+        before = pltpu.roll(turned[96:128], 1, 0)
+        after = pltpu.roll(turned[0:32], 31, 0)
+        moved = (before, jnp.where(left, before, after), after)[pair]
+        out[pl.ds(LINES + pair, GROUP, stride=SENT), :] = moved
 
 
 def transform(received):
@@ -197,12 +198,15 @@
     return out
 
 
-def weights_kernel(lengths, cells, offsets, near, side):
+def weights_kernel(lengths, cells, offsets, counts_far, near, side, counts, done):
+    copy = pltpu.make_async_copy(counts_far, counts, done)
+    copy.start()
     start_y = lax.axis_index("gy") * CELLS
     start_z = lax.axis_index("gz") * CELLS
     row = lax.broadcasted_iota(jnp.int32, (CELLS, TILE), 0)
     row_y = lax.broadcasted_iota(jnp.int32, (CELLS + 16, TILE), 0) - 8
-    edge = lax.broadcasted_iota(jnp.int32, (8, TILE), 0)
+    spot8 = lax.broadcasted_iota(jnp.int32, (8, TILE), 0)
+    edge = jnp.where(spot8 < 4, 2 * spot8, 2 * spot8 - 7)
     edge = jnp.where(edge < 3, edge - 3, jnp.where(edge < 6, edge + 125, -9999))
     blank = jnp.zeros((8, TILE), jnp.float32)
 
@@ -221,10 +225,15 @@
         for part in range(4):
             near[index, 384 + part * 32 : 416 + part * 32, :] = block.astype(jnp.bfloat16)
         side[index, 0:144, :] = spread(weights[1], row_y - first_y)
-        side[index, 144:152, :] = jnp.concatenate(weights[0] + weights[0], axis=0)
+        side[index, 144:148, :] = jnp.concatenate(weights[0], axis=0)
         return carry
 
     lax.fori_loop(0, cells.shape[1] // TILE, tile, 0)
+    copy.wait()
+    lane = lax.broadcasted_iota(jnp.int32, (4, TILE), 1)
+    for index in range(cells.shape[1] // TILE):
+        live = lane + index * TILE < counts[0]
+        side[index, 148:152, :] = jnp.where(live, 1.0, 0.0)
 
 
 def fill(wide, row, count, inner, outer):
@@ -236,20 +245,27 @@
 
 
 def turn_tails(tails):
+    row = lax.broadcasted_iota(jnp.int32, (8, CELLS), 0)
     rows = []
     for tail in tails:
-        coarse = tail.astype(jnp.bfloat16).astype(jnp.float32)
-        rows += [coarse, coarse, tail - coarse, jnp.zeros_like(tail)]
-    return jnp.concatenate(rows, axis=0).T
+        both = jnp.where(row < 4, pltpu.roll(tail, 3, 0), pltpu.roll(tail, 7, 0))
+        both = jnp.where(row % 4 == 3, 0.0, both)
+        coarse = both.astype(jnp.bfloat16).astype(jnp.float32)
+        rows += [coarse, coarse, both - coarse, jnp.zeros_like(both)]
+    turned = jnp.concatenate(rows, axis=0).T
+    lane = lax.broadcasted_iota(jnp.int32, (64, CELLS), 1)
+    return jnp.where(lane % 8 < 4, turned[:64], turned[64:])
 
 
 def block_kernel(data, near, side, coefficients, sums, wide, held):
     lane = lax.broadcasted_iota(jnp.int32, (LINES, CELLS), 1)
     for group in range(8):
-        turned = turn_tails([data[group * 4 + t, LINES:SENT, :] for t in range(4)])[:LINES]
+        turned = turn_tails(
+            [data[(group * 4 + t + 1) * SENT - 8 : (group * 4 + t + 1) * SENT, :] for t in range(4)]
+        )[:LINES]
         for t in range(4):
             whole = group * 4 + t
-            inner = data[whole, :LINES, :]
+            inner = data[whole * SENT : whole * SENT + LINES, :]
             fill(wide, whole * LINES, LINES, inner, jnp.where(lane // 32 == t, turned, 0.0))
             for c in range(3):
                 coefficients[c, whole // 8, whole % 8 * 16 : whole % 8 * 16 + 16, :] = inner[
@@ -278,26 +294,34 @@
         tile(index, index % 2)
 
 
-def edge_kernel(counts, below, above, near, side, sums, out, wide, held):
-    lane = lax.broadcasted_iota(jnp.int32, (16, CELLS), 1)
-    sides = (below, above)
+def edge_kernel(above, below, near, side, sums, out, wide, held):
+    lane = lax.broadcasted_iota(jnp.int32, (8, CELLS), 1)
+    row = lax.broadcasted_iota(jnp.int32, (8, CELLS), 0)
     parts = []
-    for group in range(2):
-        turned = turn_tails([sides[group][a, 24:32, :] for a in range(4)])
+    for group, rows in enumerate((below, above)):
+        turned = turn_tails([rows[a * 16 + 8 : a * 16 + 16, :] for a in range(4)])
         for a in range(4):
+            first, second = rows[a * 16 : a * 16 + 8, :], rows[a * 16 + 8 : a * 16 + 16, :]
             for c in range(3):
-                first = c * 16 + (8 if group == 0 else 0)
-                outer = jnp.where(lane[:8] // 32 == a, turned[first : first + 8], 0.0)
-                parts.append((sides[group][a, c * 8 : c * 8 + 8, :], outer))
+                three = first if c < 2 else second
+                used = row < 3
+                if group == 0:
+                    three, used = pltpu.roll(three, 5 - c % 2 * 3, 0), row >= 5
+                elif c == 1:
+                    three = pltpu.roll(three, 5, 0)
+                inner = jnp.where(used, three, 0.0)
+                at = c * 16 + (8 if group == 0 else 0)
+                outer = jnp.where(used & (lane // 32 == a), turned[at : at + 8], 0.0)
+                parts.append((inner, outer))
     for place in range(0, 24, 2):
         inner, outer = [jnp.concatenate(pair, axis=0) for pair in zip(*parts[place : place + 2])]
         fill(wide, place * 8, 16, inner, outer)
     for index in range(near.shape[0]):
         at = index * TILE
         held[index] = jnp.dot(wide[...], near[index], preferred_element_type=jnp.float32)
+        live = side[index, 148:149, :] > 0.5
         low = side[index, 0:8, :]
         high = side[index, 136:144, :]
-        slot = at + lax.broadcasted_iota(jnp.int32, (1, TILE), 1)
         for c in range(3):
             total = None
             for a in range(4):
@@ -307,32 +331,54 @@
                 ) * side[index, 144 + a : 145 + a, :]
                 total = term if total is None else total + term
             value = sums[c : c + 1, at : at + TILE] + jnp.sum(total, axis=0, keepdims=True)
-            out[c : c + 1, at : at + TILE] = jnp.where(slot < counts[0:1, 0:1], value, 0.0)
+            out[c : c + 1, at : at + TILE] = jnp.where(live, value, 0.0)
 
 
 def vmem():
     return pl.BlockSpec(memory_space=pltpu.VMEM)
 
 
-def particle_weights(lengths, cells, offsets):
+def rims_kernel(data, bottom, top):
+    for a in range(4):
+        for out, first, low in ((bottom, a * 8 * SENT, 0), (top, (a * 8 + 7) * SENT, 13)):
+            rows = [data[first + c * 16 + low : first + c * 16 + low + 3, :] for c in range(3)]
+            rows.append(data[first + 46 : first + SENT, :])
+            for place, part in zip((0, 3, 8, 11), rows):
+                out[a * 16 + place : a * 16 + place + part.shape[0], :] = part
+            out[a * 16 + 6 : a * 16 + 8, :] = jnp.zeros((2, CELLS), jnp.float32)
+
+
+def rims(owned):
+    return pl.pallas_call(
+        rims_kernel,
+        in_specs=[vmem()],
+        out_specs=[vmem()] * 2,
+        out_shape=[jax.ShapeDtypeStruct((64, CELLS), jnp.float32)] * 2,
+        compiler_params=pltpu.CompilerParams(vmem_limit_bytes=4 * MIB),
+        name="rims",
+    )(owned)
+
+
+def particle_weights(lengths, cells, offsets, counts):
     def body(*refs):
         weights_kernel(lengths, *refs)
 
     count = cells.shape[1] // TILE
     return pl.pallas_call(
         body,
-        in_specs=[vmem()] * 2,
+        in_specs=[vmem()] * 2 + [pl.BlockSpec(memory_space=pl.ANY)],
         out_specs=[vmem()] * 2,
         out_shape=[
             jax.ShapeDtypeStruct((count, 512, TILE), jnp.bfloat16),
             jax.ShapeDtypeStruct((count, CELLS + 24, TILE), jnp.float32),
         ],
+        scratch_shapes=[pltpu.SMEM((1,), jnp.int32), pltpu.SemaphoreType.DMA],
         compiler_params=pltpu.CompilerParams(vmem_limit_bytes=10 * MIB),
         cost_estimate=pl.CostEstimate(
             flops=10_000_000, bytes_accessed=4_000_000, transcendentals=0
         ),
         name="weights",
-    )(cells, offsets)
+    )(cells, offsets, counts)
 
 
 def interpolate_block(data, near, side):
@@ -354,10 +400,10 @@
     )(data, near, side)
 
 
-def interpolate_edges(counts, below, above, near, side, sums):
+def interpolate_edges(above, below, near, side, sums):
     return pl.pallas_call(
         edge_kernel,
-        in_specs=[vmem()] * 6,
+        in_specs=[vmem()] * 5,
         out_specs=vmem(),
         out_shape=jax.ShapeDtypeStruct(sums.shape, jnp.float32),
         scratch_shapes=[
@@ -366,7 +412,7 @@
         ],
         compiler_params=pltpu.CompilerParams(vmem_limit_bytes=10 * MIB),
         name="edges",
-    )(counts, below, above, near, side, sums)
+    )(above, below, near, side, sums)
 
 
 def per_device(spectrum, cells, offsets, counts):
@@ -377,18 +423,17 @@
     received = lax.all_to_all(
         by_target.reshape(GROUP, 96, CELLS), "gz", split_axis=0, concat_axis=0, tiled=True
     )
-    lines = transform(received).reshape(GROUP, SENT, CELLS)
+    lines = transform(received).reshape(GROUP, SENT, 1, CELLS)
     owned = lax.all_to_all(lines, "gz", split_axis=0, concat_axis=0, tiled=True)
-    tiles = owned.reshape(4, 8, 7, 8, CELLS)
-    top = jnp.stack([tiles[:, 7, i] for i in (1, 3, 5, 6)], axis=1).reshape(4, 32, CELLS)
-    bottom = jnp.stack([tiles[:, 0, i] for i in (0, 2, 4, 6)], axis=1).reshape(4, 32, CELLS)
+    owned = owned.reshape(GROUP * SENT, CELLS)
+    bottom, top = rims(owned)
     forward = [(i, (i + 1) % count_y) for i in range(count_y)]
     backward = [(target, source) for source, target in forward]
     above = lax.ppermute(bottom, "gy", backward)
     below = lax.ppermute(top, "gy", forward)
-    near, side = particle_weights(lengths, cells, offsets)
+    near, side = particle_weights(lengths, cells, offsets, counts)
     coefficients, sums = interpolate_block(owned, near, side)
-    interpolated = interpolate_edges(counts.reshape(1, 1), below, above, near, side, sums)
+    interpolated = interpolate_edges(above, below, near, side, sums)
     return coefficients, interpolated
 
 

time: 96.6 us -> 94 us (0.973)
  blocking collectives: 78.2 us -> 76.7 us
    all_to_all x1, blocking collectives: 29.7 us -> 28.3 us  [per_device(): owned = lax.all_to_all(lines, 'gz', split_axis=0, concat_axis=0, tiled=True)]
    pallas_call x2 -> x3, Pallas kernels: 2.25 us -> 2.29 us  [the longest x1 1.25 us: interpolate_edges(): pl.pallas_call(edge_kernel, in_specs=[vmem()] * 5, out_specs=vmem(), out_...]
where the time goes in v3:
time: 94 us; the launch traced here: 93.8 us
  blocking collectives  76.7 us (82%)
  Pallas kernels  7.86 us (8%)
  starting transfers between devices  6.2 us (7%)
  local copies, waits for them, and re-layouts  1.63 us (2%)
  between operations  1.38 us (1%)
    all_to_all x1, blocking collectives, per_device(): lax.all_to_all(by_target.reshape(GROUP, 96, CELLS), 'gz', split_axis=0, c...  48.5 us
    all_to_all x1, blocking collectives, per_device(): owned = lax.all_to_all(lines, 'gz', split_axis=0, concat_axis=0, tiled=True)  28.3 us
    ppermute x1, starting transfers between devices, per_device(): above = lax.ppermute(bottom, 'gy', backward)  5 us
    pallas_call x1, Pallas kernels, interpolate_block(): pl.pallas_call(block_kernel, in_specs=[vmem()] * 3, out_specs=[vmem()] *...  3.47 us
    pallas_call x1, Pallas kernels, transform(): pl.pallas_call(lines_kernel, out_shape=jax.ShapeDtypeStruct((GROUP * SENT...  2.1 us
  transfers between devices with their start and end apart: 2, of which 0 were waited for; matrix products, arithmetic and copies ran while one was open for 0% of the time, Pallas kernels for 5%

profile of v3, /device:TPU:1, one launch (start us, length us, event | category | flops | bytes accessed | tf_op | source)
XLA Modules:
  0.0 93.8 jit_solution(15743342451721038601)
XLA Ops:
  0.6 1.6 %copy.10 = f32[6,32,16,128]{3,2,0,1:T(8,128)S(1)} copy(f32[6,32,16,128]{3,2,1,0:T(8,128)} %bitcast.10) | data formatting | bytes 3145728 | tf_op jit(solution)/shard_map/reshape | solution.py:422
  2.2 0.0 copy-start
  2.3 0.0 copy-start.1
  2.3 48.5 %all_to_all.10.data = f32[32,96,128]{2,1,0:T(8,128)S(1)} all-to-all(f32[32,96,128]{2,1,0:T(8,128)S(1)} %bitcast.9), channel_id=1, replica_groups=mesh['gz'=32,'gy'=8] {'gz'}, dimensions={0} | all-to-all | bytes 3145728 | tf_op jit(solution)/shard_map/all_to_all | solution.py:423
  50.7 0.0 copy-done
  50.7 0.0 copy-done.1
  50.7 2.1 %lines.1 = f32[1632,128]{1,0:T(8,128)S(1)} custom-call(f32[32,96,128]{2,1,0:T(8,128)S(1)} %all_to_all.10.data, f32[3,32,128]{2,1,0:T(8,128)S(1)} %copy-done.1, bf16[768,128]{1,0:T(8,128)(2,1)S(1)} %copy-done), custom_call_target="tpu_custom_call" | custom-call | tf_op jit(solution)/shard_map/lines/pallas_call | solution.py:170
  52.8 0.0 copy-start.2
  52.9 0.0 copy-start.3
  52.9 28.3 %all_to_all.11 = f32[32,51,1,128]{3,2,1,0:T(1,128)S(1)} all-to-all(f32[32,51,1,128]{3,2,1,0:T(1,128)S(1)} %bitcast.8), channel_id=1, replica_groups=mesh['gz'=32,'gy'=8] {'gz'}, dimensions={0} | all-to-all | bytes 1671168 | tf_op jit(solution)/shard_map/all_to_all | solution.py:427
  81.1 5.0 %collective-permute-start = (f32[64,128]{1,0:T(8,128)S(1)}, f32[64,128]{1,0:T(8,128)S(1)}, u32[]{:S(2)}, u32[]{:S(2)}) collective-permute-start(f32[64,128]{1,0:T(8,128)S(1)} %get-tuple-element.11), channel_id=1, source_target_pairs={{1,0},{2,1},{3,2},{4,3},{5,4},{6,5},{7,6},{0,7},{9,8},{10,9},{11,1... | collective-permute-start | bytes 98312 | tf_op jit(solution)/shard_map/ppermute | solution.py:432
  86.1 1.2 %collective-permute-start.1 = (f32[64,128]{1,0:T(8,128)S(1)}, f32[64,128]{1,0:T(8,128)S(1)}, u32[]{:S(2)}, u32[]{:S(2)}) collective-permute-start(f32[64,128]{1,0:T(8,128)S(1)} %get-tuple-element.12), channel_id=1, source_target_pairs={{0,1},{1,2},{2,3},{3,4},{4,5},{5,6},{6,7},{7,0},{8,9},{9,10},{10,1... | collective-permute-start | bytes 98312 | tf_op jit(solution)/shard_map/ppermute | solution.py:433
  88.0 0.0 copy-done.2
  88.0 0.0 copy-done.3
  88.0 1.0 %weights.1 = (bf16[8,512,256]{2,1,0:T(8,128)(2,1)S(1)}, f32[8,152,256]{2,1,0:T(8,128)S(1)}) custom-call(s32[2,2048]{1,0:T(2,128)S(1)} %copy-done.3, f32[3,2048]{1,0:T(4,128)S(1)} %copy-done.2, s32[1]{0:T(128)S(6)} %copy.12.refs_2_), custom_call_target="tpu_custom_call" | custom-call | flops 10000000 | bytes 4000000 | tf_op jit(solution)/shard_map/weights/pallas_call | solution.py:367
  89.0 3.5 %block.1 = (f32[3,4,128,128]{3,2,1,0:T(8,128)}, f32[3,2048]{1,0:T(4,128)S(1)}) custom-call(f32[1632,128]{1,0:T(8,128)S(1)} %bitcast.7, bf16[8,512,256]{2,1,0:T(8,128)(2,1)S(1)} %get-tuple-element.8.near, f32[8,152,256]{2,1,0:T(8,128)S(1)} %get-tuple-element.9.side), custom_call_target="tpu_custom_call" | custom-call | tf_op jit(solution)/shard_map/block/pallas_call | solution.py:386
  92.5 0.0 collective-permute-done.above
  92.5 0.0 collective-permute-done.1.below
  92.5 1.3 %edges.1 = f32[3,2048]{1,0:T(4,128)} custom-call(f32[64,128]{1,0:T(8,128)S(1)} %collective-permute-done.above, f32[64,128]{1,0:T(8,128)S(1)} %collective-permute-done.1.below, bf16[8,512,256]{2,1,0:T(8,128)(2,1)S(1)} %get-tuple-element.8.near, f32[8,152,256]{2,1,0:T(8,128)S(1)} %get-tuple-element.9.side, f32[3,2048]{1,0:T(4,128)S(1)} %get-tuple-element.13.sums), custom_call_target="tpu_custom_call" | custom-call | tf_op jit(solution)/shard_map/edges/pallas_call | solution.py:404
  (1 shorter events, 0.0 us)
Async XLA Ops:
  2.2 48.5 %copy-start = (bf16[768,128]{1,0:T(8,128)(2,1)S(1)}, bf16[768,128]{1,0:T(8,128)(2,1)}, u32[]{:S(2)}) copy-start(bf16[768,128]{1,0:T(8,128)(2,1)} %constant.5.clone.matrix) | copy-start | bytes 589828
  2.3 48.5 %copy-start.1 = (f32[3,32,128]{2,1,0:T(8,128)S(1)}, f32[3,32,128]{2,1,0:T(8,128)}, u32[]{:S(2)}) copy-start(f32[3,32,128]{2,1,0:T(8,128)} %constant.4.clone.table) | copy-start | bytes 147460
  52.8 35.2 %copy-start.2 = (f32[3,2048]{1,0:T(4,128)S(1)}, f32[3,2048]{1,0:T(4,128)}, u32[]{:S(2)}) copy-start(f32[3,2048]{1,0:T(4,128)} %refs_1_.1) | copy-start | bytes 73732
  52.9 35.2 %copy-start.3 = (s32[2,2048]{1,0:T(2,128)S(1)}, s32[2,2048]{1,0:T(2,128)}, u32[]{:S(2)}) copy-start(s32[2,2048]{1,0:T(2,128)} %refs_0_.1) | copy-start | bytes 49156
  81.1 11.4 %collective-permute-start = (f32[64,128]{1,0:T(8,128)S(1)}, f32[64,128]{1,0:T(8,128)S(1)}, u32[]{:S(2)}, u32[]{:S(2)}) collective-permute-start(f32[64,128]{1,0:T(8,128)S(1)} %get-tuple-element.11), channel_id=1, source_target_pairs={{1,0},{2,1},{3,2},{4,3},{5,4},{6,5},{7,6},{0,7},{9,8},{10,9},{11,1... | collective-permute-start | bytes 98312 | tf_op jit(solution)/shard_map/ppermute | solution.py:432
  86.1 6.4 %collective-permute-start.1 = (f32[64,128]{1,0:T(8,128)S(1)}, f32[64,128]{1,0:T(8,128)S(1)}, u32[]{:S(2)}, u32[]{:S(2)}) collective-permute-start(f32[64,128]{1,0:T(8,128)S(1)} %get-tuple-element.12), channel_id=1, source_target_pairs={{0,1},{1,2},{2,3},{3,4},{4,5},{5,6},{6,7},{7,0},{8,9},{9,10},{10,1... | collective-permute-start | bytes 98312 | tf_op jit(solution)/shard_map/ppermute | solution.py:433

commit v4 on v3

--- a/solution.py
+++ b/solution.py
@@ -14,6 +14,7 @@
 SENT = 51
 TILE = 256
 MIB = 1024 * 1024
+HOPS = 3
 
 
 def split(value):
@@ -84,72 +85,77 @@
     return [add(e, o) for e, o in zip(even, odd)] + [sub(e, o) for e, o in zip(even, odd)]
 
 
-def dft32(items):
-    firsts = []
-    for j in range(8):
-        four = dft4(items[j], items[j + 8], items[j + 16], items[j + 24])
-        firsts.append([turn(item, j * r, 32) for r, item in enumerate(four)])
-    out = [None] * 32
-    for r in range(4):
-        for q, item in enumerate(dft8([firsts[j][r] for j in range(8)])):
-            out[r + 4 * q] = item
-    return out
-
-
 def lines_kernel(data, table, matrix, out, wide, flat):
-    def columns(index, carry):
-        base = index // 2 * 32 + index % 2 * 8
-        base_imag = base + 16
-        items = []
-        for k1 in range(GROUP):
-            scale = table[0, k1 : k1 + 1, :]
-            items.append(
-                (data[k1, pl.ds(base, 8), :] * scale, data[k1, pl.ds(base_imag, 8), :] * scale)
-            )
-        pair = []
-        for m, item in enumerate(dft32(items)):
-            cos, sin = table[1, m : m + 1, :], table[2, m : m + 1, :]
-            pair.append((item[0] * cos - item[1] * sin, item[0] * sin + item[1] * cos))
-            if m % 2 == 1:
-                row = index * 256 + m * 8 - 8
-                real, imag = [jnp.concatenate(parts, axis=0) for parts in zip(*pair)]
-                for at, part in ((0, real), (CELLS, imag)):
-                    high, low = split(part)
-                    wide[pl.ds(row, 16), at : at + CELLS] = high
-                    wide[pl.ds(row, 16), at + 256 : at + 256 + CELLS] = high
-                    wide[pl.ds(row, 16), at + 512 : at + 512 + CELLS] = low
-                pair = []
-        return carry
-
-    for index in range(6):
-        columns(index, 0)
-    flat[...] = jnp.dot(wide[...], matrix[...], preferred_element_type=jnp.float32)
     lane = lax.broadcasted_iota(jnp.int32, (GROUP, CELLS), 1)
     odd = lane // 32 % 2 == 1
     upper = lane // 64 == 1
+
+    def firsts_of(index):
+        base = index // 2 * 32 + index % 2 * 8
+
+        def item(k1):
+            scale = table[0, k1 : k1 + 1, :]
+            return data[k1, base : base + 8, :] * scale, data[k1, base + 16 : base + 24, :] * scale
+
+        firsts = []
+        for j in range(8):
+            four = dft4(*[item(j + 8 * step) for step in range(4)])
+            firsts.append([turn(value, j * r, 32) for r, value in enumerate(four)])
+        return firsts
+
+    def seconds_of(index, firsts, low):
+        both = []
+        for r in (low, low + 1):
+            values = dft8([firsts[j][r] for j in range(8)])
+            turned = []
+            for q, value in enumerate(values):
+                m = r + 4 * q
+                cos, sin = table[1, m : m + 1, :], table[2, m : m + 1, :]
+                turned.append((value[0] * cos - value[1] * sin, value[0] * sin + value[1] * cos))
+            both.append(turned)
+        for q in range(8):
+            row = index * 256 + (low + 4 * q) * 8
+            for at, half in ((0, 0), (CELLS, 1)):
+                part = jnp.concatenate([both[0][q][half], both[1][q][half]], axis=0)
+                high, low_part = split(part)
+                wide[row : row + 16, at : at + CELLS] = high
+                wide[row : row + 16, at + 256 : at + 256 + CELLS] = high
+                wide[row : row + 16, at + 512 : at + 512 + CELLS] = low_part
+
+    def place(index, half):
+        rows = [
+            flat[pl.ds(index * 256 + half * 4 + line, GROUP, stride=8), :] for line in range(4)
+        ]
+        turned = jnp.concatenate(rows, axis=0).T
+        v = [turned[s * 32 : s * 32 + 32] for s in range(4)]
+        w = [
+            jnp.where(odd, pltpu.roll(v[1], 32, 1), v[0]),
+            jnp.where(odd, v[1], pltpu.roll(v[0], 96, 1)),
+            jnp.where(odd, pltpu.roll(v[3], 32, 1), v[2]),
+            jnp.where(odd, v[3], pltpu.roll(v[2], 96, 1)),
+        ]
+        o = [
+            jnp.where(upper, pltpu.roll(w[2], 64, 1), w[0]),
+            jnp.where(upper, pltpu.roll(w[3], 64, 1), w[1]),
+            jnp.where(upper, w[2], pltpu.roll(w[0], 64, 1)),
+            jnp.where(upper, w[3], pltpu.roll(w[1], 64, 1)),
+        ]
+        for line in range(4):
+            row = index * 8 + half * 4 + line
+            out[pl.ds(row, GROUP, stride=SENT), :] = o[line]
+
     for index in range(6):
-        for half in range(2):
-            rows = [
-                flat[pl.ds(index * 256 + half * 4 + line, GROUP, stride=8), :]
-                for line in range(4)
-            ]
-            turned = jnp.concatenate(rows, axis=0).T
-            v = [turned[s * 32 : s * 32 + 32] for s in range(4)]
-            w = [
-                jnp.where(odd, pltpu.roll(v[1], 32, 1), v[0]),
-                jnp.where(odd, v[1], pltpu.roll(v[0], 96, 1)),
-                jnp.where(odd, pltpu.roll(v[3], 32, 1), v[2]),
-                jnp.where(odd, v[3], pltpu.roll(v[2], 96, 1)),
-            ]
-            o = [
-                jnp.where(upper, pltpu.roll(w[2], 64, 1), w[0]),
-                jnp.where(upper, pltpu.roll(w[3], 64, 1), w[1]),
-                jnp.where(upper, w[2], pltpu.roll(w[0], 64, 1)),
-                jnp.where(upper, w[3], pltpu.roll(w[1], 64, 1)),
-            ]
-            for line in range(4):
-                row = index * 8 + half * 4 + line
-                out[pl.ds(row, GROUP, stride=SENT), :] = o[line]
+        firsts = firsts_of(index)
+        if index:
+            place(index - 1, 0)
+        seconds_of(index, firsts, 0)
+        if index:
+            place(index - 1, 1)
+        seconds_of(index, firsts, 2)
+        part = slice(index * 256, index * 256 + 256)
+        flat[part, :] = jnp.dot(wide[part, :], matrix[...], preferred_element_type=jnp.float32)
+    place(5, 0)
+    place(5, 1)
     empty = jnp.zeros((16, CELLS), jnp.float32)
     left = lax.broadcasted_iota(jnp.int32, (GROUP, CELLS), 1) < 64
     for pair in range(3):
@@ -415,11 +421,25 @@
     )(above, below, near, side, sums)
 
 
+def wait_for_turn(token):
+    count = lax.axis_size("gy")
+    token = token[:1, :CELLS]
+    for _ in range(HOPS):
+        token = lax.ppermute(
+            token, "gy", [(i, (i + 2) % count) for i in range(1, count, 2)]
+        )
+    return token[0, 0]
+
+
 def per_device(spectrum, cells, offsets, counts):
     rows_y, rows_z = spectrum.shape[3], spectrum.shape[4]
     count_y, count_z = lax.axis_size("gy"), lax.axis_size("gz")
     lengths = (rows_y * count_y, rows_z * count_z)
     by_target = spectrum.reshape(6, GROUP, 16, CELLS).transpose(1, 0, 2, 3)
+    turn_of = lax.cond(
+        (lax.axis_index("gy") & 1) == 1, wait_for_turn, lambda _: jnp.float32(0.0), offsets
+    )
+    by_target = jnp.where(turn_of != turn_of, 0.0, by_target)
     received = lax.all_to_all(
         by_target.reshape(GROUP, 96, CELLS), "gz", split_axis=0, concat_axis=0, tiled=True
     )

time: 94 us -> 88.1 us (0.937)
  blocking collectives: 76.7 us -> 57 us
  waiting for transfers between devices: 0.01 us -> 9.49 us
  starting transfers between devices: 6.2 us -> 9.59 us
  other arithmetic: 0 us -> 1.52 us
    all_to_all x1, blocking collectives: 48.5 us -> 34.9 us  [per_device(): lax.all_to_all(by_target.reshape(GROUP, 96, CELLS), 'gz', split_axis=0, c...]
    ppermute x0 -> x3, waiting for transfers between devices: none -> 9.48 us  [wait_for_turn(): lax.ppermute(token, 'gy', [(i, (i + 2) % count) for i in range(1, count,...]
    ppermute x0 -> x3, starting transfers between devices: none -> 7.84 us  [wait_for_turn(): lax.ppermute(token, 'gy', [(i, (i + 2) % count) for i in range(1, count,...]
    all_to_all x1, blocking collectives: 28.3 us -> 22.1 us  [per_device(): owned = lax.all_to_all(lines, 'gz', split_axis=0, concat_axis=0, tiled=True)]
    ppermute x1, starting transfers between devices: 5 us -> 0.02 us  [per_device(): above = lax.ppermute(bottom, 'gy', backward)]
    reshape x1 -> x0, local copies, waits for them, and re-layouts: 1.6 us -> none  [per_device(): by_target = spectrum.reshape(6, GROUP, 16, CELLS).transpose(1, 0, 2, 3)]
    select_n x0 -> x1, other arithmetic: none -> 1.52 us  [per_device(): by_target = jnp.where(turn_of != turn_of, 0.0, by_target)]
  transfers between devices with their start and end apart: 2 -> 5, of which waited for: 0 -> 3; matrix products, arithmetic and copies ran while one was open for 0% -> 0% of each run, Pallas kernels for 5% -> 5%
where the time goes in v4:
time: 88.1 us; the launch traced here: 87.7 us
  blocking collectives  57 us (65%)
  starting transfers between devices  9.59 us (11%)
  waiting for transfers between devices  9.49 us (11%)
  Pallas kernels  7.74 us (9%)
  other arithmetic  1.52 us (2%)
  between operations  1.41 us (2%)
  local copies, waits for them, and re-layouts  0.91 us (1%)
    all_to_all x1, blocking collectives, per_device(): lax.all_to_all(by_target.reshape(GROUP, 96, CELLS), 'gz', split_axis=0, c...  34.9 us
    all_to_all x1, blocking collectives, per_device(): owned = lax.all_to_all(lines, 'gz', split_axis=0, concat_axis=0, tiled=True)  22.1 us
    ppermute x3, waiting for transfers between devices, wait_for_turn(): lax.ppermute(token, 'gy', [(i, (i + 2) % count) for i in range(1, count,...  9.48 us
    ppermute x3, starting transfers between devices, wait_for_turn(): lax.ppermute(token, 'gy', [(i, (i + 2) % count) for i in range(1, count,...  7.84 us
    pallas_call x1, Pallas kernels, interpolate_block(): pl.pallas_call(block_kernel, in_specs=[vmem()] * 3, out_specs=[vmem()] *...  3.47 us
    pallas_call x1, Pallas kernels, transform(): pl.pallas_call(lines_kernel, out_shape=jax.ShapeDtypeStruct((GROUP * SENT...  1.98 us
  transfers between devices with their start and end apart: 5, of which 3 were waited for; matrix products, arithmetic and copies ran while one was open for 0% of the time, Pallas kernels for 5%

profile of v4, /device:TPU:1, one launch (start us, length us, event | category | flops | bytes accessed | tf_op | source)
XLA Modules:
  0.0 87.7 jit_solution(6473244429417305604)
XLA Ops:
  0.6 18.1 %conditional.1 = (pred[]{:T(512)}) conditional(s32[]{:T(128)} %convert_element_type.3, () %tuple.14, f32[3,2048]{1,0:T(4,128)} %refs_1_.1), branch_computations={%region_0.0_spmd, %region_1.0_spmd} | conditional | flops 1 | bytes 7305 | solution.py:439
  0.6 0.7 slice.4
  1.3 4.0 %collective-permute-start = (f32[1,128]{1,0:T(1,128)S(1)}, f32[1,128]{1,0:T(1,128)S(1)}, u32[]{:S(2)}, u32[]{:S(2)}) collective-permute-start(f32[1,128]{1,0:T(1,128)S(1)} %slice.4), channel_id=1, source_target_pairs={{1,3},{3,5},{5,7},{7,1},{9,11},{11,13},{13,15},{15,9},{17,19},{19,... | collective-permute-start | bytes 1544 | tf_op jit(solution)/shard_map/cond/branch_1_fun/ppermute | solution.py:428
  5.4 2.4 %collective-permute-done = f32[1,128]{1,0:T(1,128)S(1)} collective-permute-done((f32[1,128]{1,0:T(1,128)S(1)}, f32[1,128]{1,0:T(1,128)S(1)}, u32[]{:S(2)}, u32[]{:S(2)}) %collective-permute-start) | collective-permute-done | bytes 544 | tf_op jit(solution)/shard_map/cond/branch_1_fun/ppermute | solution.py:428
  7.7 1.9 %collective-permute-start.1 = (f32[1,128]{1,0:T(1,128)S(1)}, f32[1,128]{1,0:T(1,128)S(1)}, u32[]{:S(2)}, u32[]{:S(2)}) collective-permute-start(f32[1,128]{1,0:T(1,128)S(1)} %collective-permute-done), channel_id=1, source_target_pairs={{1,3},{3,5},{5,7},{7,1},{9,11},{11,13},{13,15},{15,9},{17,19},{19,... | collective-permute-start | bytes 1544 | tf_op jit(solution)/shard_map/cond/branch_1_fun/ppermute | solution.py:428
  9.6 3.6 %collective-permute-done.1 = f32[1,128]{1,0:T(1,128)S(1)} collective-permute-done((f32[1,128]{1,0:T(1,128)S(1)}, f32[1,128]{1,0:T(1,128)S(1)}, u32[]{:S(2)}, u32[]{:S(2)}) %collective-permute-start.1) | collective-permute-done | bytes 544 | tf_op jit(solution)/shard_map/cond/branch_1_fun/ppermute | solution.py:428
  13.2 1.9 %collective-permute-start.2 = (f32[1,128]{1,0:T(1,128)S(1)}, f32[1,128]{1,0:T(1,128)S(1)}, u32[]{:S(2)}, u32[]{:S(2)}) collective-permute-start(f32[1,128]{1,0:T(1,128)S(1)} %collective-permute-done.1), channel_id=1, source_target_pairs={{1,3},{3,5},{5,7},{7,1},{9,11},{11,13},{13,15},{15,9},{17,19},{19,... | collective-permute-start | bytes 1544 | tf_op jit(solution)/shard_map/cond/branch_1_fun/ppermute | solution.py:428
  15.1 3.6 %collective-permute-done.2 = f32[1,128]{1,0:T(1,128)S(1)} collective-permute-done((f32[1,128]{1,0:T(1,128)S(1)}, f32[1,128]{1,0:T(1,128)S(1)}, u32[]{:S(2)}, u32[]{:S(2)}) %collective-permute-start.2) | collective-permute-done | bytes 544 | tf_op jit(solution)/shard_map/cond/branch_1_fun/ppermute | solution.py:428
  18.7 1.5 %broadcast_select_fusion = f32[3,2,4,128,128]{4,3,2,1,0:T(8,128)S(1)} fusion(f32[3,2,4,128,128]{4,3,2,1,0:T(8,128)} %param.8, pred[]{:T(512)} %get-tuple-element.18), kind=kLoop, calls=%fused_computation | loop fusion | flops 393216 | bytes 3145729 | tf_op jit(solution)/shard_map/jit(_where)/select_n | solution.py:442
  20.3 0.2 copy.10
  20.5 0.0 copy-start
  20.5 0.0 copy-start.1
  20.5 34.9 %all_to_all.10.data = f32[32,96,128]{2,1,0:T(8,128)S(1)} all-to-all(f32[32,96,128]{2,1,0:T(8,128)S(1)} %bitcast.11), channel_id=1, replica_groups=mesh['gz'=32,'gy'=8] {'gz'}, dimensions={0} | all-to-all | bytes 3145728 | tf_op jit(solution)/shard_map/all_to_all | solution.py:443
  55.4 0.0 copy-done
  55.4 0.0 copy-done.1
  55.4 2.0 %lines.1 = f32[1632,128]{1,0:T(8,128)S(1)} custom-call(f32[32,96,128]{2,1,0:T(8,128)S(1)} %all_to_all.10.data, f32[3,32,128]{2,1,0:T(8,128)S(1)} %copy-done.1, bf16[768,128]{1,0:T(8,128)(2,1)S(1)} %copy-done), custom_call_target="tpu_custom_call" | custom-call | tf_op jit(solution)/shard_map/lines/pallas_call | solution.py:176
  57.4 0.0 copy-start.2
  57.4 0.0 copy-start.3
  57.4 22.1 %all_to_all.11 = f32[32,51,1,128]{3,2,1,0:T(1,128)S(1)} all-to-all(f32[32,51,1,128]{3,2,1,0:T(1,128)S(1)} %bitcast.10), channel_id=1, replica_groups=mesh['gz'=32,'gy'=8] {'gz'}, dimensions={0} | all-to-all | bytes 1671168 | tf_op jit(solution)/shard_map/all_to_all | solution.py:447
  79.5 0.0 collective-permute-start.3
  79.6 1.7 %collective-permute-start.4 = (f32[64,128]{1,0:T(8,128)S(1)}, f32[64,128]{1,0:T(8,128)S(1)}, u32[]{:S(2)}, u32[]{:S(2)}) collective-permute-start(f32[64,128]{1,0:T(8,128)S(1)} %get-tuple-element.16), channel_id=1, source_target_pairs={{0,1},{1,2},{2,3},{3,4},{4,5},{5,6},{6,7},{7,0},{8,9},{9,10},{10,1... | collective-permute-start | bytes 98312 | tf_op jit(solution)/shard_map/ppermute | solution.py:453
  81.9 0.0 copy-done.2
  81.9 0.0 copy-done.3
  82.0 1.0 %weights.1 = (bf16[8,512,256]{2,1,0:T(8,128)(2,1)S(1)}, f32[8,152,256]{2,1,0:T(8,128)S(1)}) custom-call(s32[2,2048]{1,0:T(2,128)S(1)} %copy-done.2, f32[3,2048]{1,0:T(4,128)S(1)} %copy-done.3, s32[1]{0:T(128)S(6)} %copy.15.refs_2_), custom_call_target="tpu_custom_call" | custom-call | flops 10000000 | bytes 4000000 | tf_op jit(solution)/shard_map/weights/pallas_call | solution.py:373
  83.0 3.5 %block.1 = (f32[3,4,128,128]{3,2,1,0:T(8,128)}, f32[3,2048]{1,0:T(4,128)S(1)}) custom-call(f32[1632,128]{1,0:T(8,128)S(1)} %bitcast.9, bf16[8,512,256]{2,1,0:T(8,128)(2,1)S(1)} %get-tuple-element.12.near, f32[8,152,256]{2,1,0:T(8,128)S(1)} %get-tuple-element.13.side), custom_call_target="tpu_custom_call" | custom-call | tf_op jit(solution)/shard_map/block/pallas_call | solution.py:392
  86.5 0.0 collective-permute-done.3.above
  86.5 0.0 collective-permute-done.4.below
  86.5 1.3 %edges.1 = f32[3,2048]{1,0:T(4,128)} custom-call(f32[64,128]{1,0:T(8,128)S(1)} %collective-permute-done.3.above, f32[64,128]{1,0:T(8,128)S(1)} %collective-permute-done.4.below, bf16[8,512,256]{2,1,0:T(8,128)(2,1)S(1)} %get-tuple-element.12.near, f32[8,152,256]{2,1,0:T(8,128)S(1)} %get-tuple-element.13.side, f32[3,2048]{1,0:T(4,128)S(1)} %get-tuple-element.17.sums), custom_call_target="tpu_custom_call" | custom-call | tf_op jit(solution)/shard_map/edges/pallas_call | solution.py:410
  (1 shorter events, 0.0 us)
Async XLA Ops:
  1.3 6.4 %collective-permute-start = (f32[1,128]{1,0:T(1,128)S(1)}, f32[1,128]{1,0:T(1,128)S(1)}, u32[]{:S(2)}, u32[]{:S(2)}) collective-permute-start(f32[1,128]{1,0:T(1,128)S(1)} %slice.4), channel_id=1, source_target_pairs={{1,3},{3,5},{5,7},{7,1},{9,11},{11,13},{13,15},{15,9},{17,19},{19,... | collective-permute-start | bytes 1544 | tf_op jit(solution)/shard_map/cond/branch_1_fun/ppermute | solution.py:428
  7.7 5.5 %collective-permute-start.1 = (f32[1,128]{1,0:T(1,128)S(1)}, f32[1,128]{1,0:T(1,128)S(1)}, u32[]{:S(2)}, u32[]{:S(2)}) collective-permute-start(f32[1,128]{1,0:T(1,128)S(1)} %collective-permute-done), channel_id=1, source_target_pairs={{1,3},{3,5},{5,7},{7,1},{9,11},{11,13},{13,15},{15,9},{17,19},{19,... | collective-permute-start | bytes 1544 | tf_op jit(solution)/shard_map/cond/branch_1_fun/ppermute | solution.py:428
  13.2 5.5 %collective-permute-start.2 = (f32[1,128]{1,0:T(1,128)S(1)}, f32[1,128]{1,0:T(1,128)S(1)}, u32[]{:S(2)}, u32[]{:S(2)}) collective-permute-start(f32[1,128]{1,0:T(1,128)S(1)} %collective-permute-done.1), channel_id=1, source_target_pairs={{1,3},{3,5},{5,7},{7,1},{9,11},{11,13},{13,15},{15,9},{17,19},{19,... | collective-permute-start | bytes 1544 | tf_op jit(solution)/shard_map/cond/branch_1_fun/ppermute | solution.py:428
  20.5 35.0 %copy-start = (bf16[768,128]{1,0:T(8,128)(2,1)S(1)}, bf16[768,128]{1,0:T(8,128)(2,1)}, u32[]{:S(2)}) copy-start(bf16[768,128]{1,0:T(8,128)(2,1)} %constant.15.clone.matrix) | copy-start | bytes 589828
  20.5 35.0 %copy-start.1 = (f32[3,32,128]{2,1,0:T(8,128)S(1)}, f32[3,32,128]{2,1,0:T(8,128)}, u32[]{:S(2)}) copy-start(f32[3,32,128]{2,1,0:T(8,128)} %constant.14.clone.table) | copy-start | bytes 147460
  57.4 24.5 %copy-start.2 = (s32[2,2048]{1,0:T(2,128)S(1)}, s32[2,2048]{1,0:T(2,128)}, u32[]{:S(2)}) copy-start(s32[2,2048]{1,0:T(2,128)} %refs_0_.1) | copy-start | bytes 49156
  57.4 24.5 %copy-start.3 = (f32[3,2048]{1,0:T(4,128)S(1)}, f32[3,2048]{1,0:T(4,128)}, u32[]{:S(2)}) copy-start(f32[3,2048]{1,0:T(4,128)} %refs_1_.1) | copy-start | bytes 73732
  79.5 6.9 %collective-permute-start.3 = (f32[64,128]{1,0:T(8,128)S(1)}, f32[64,128]{1,0:T(8,128)S(1)}, u32[]{:S(2)}, u32[]{:S(2)}) collective-permute-start(f32[64,128]{1,0:T(8,128)S(1)} %get-tuple-element.15), channel_id=1, source_target_pairs={{1,0},{2,1},{3,2},{4,3},{5,4},{6,5},{7,6},{0,7},{9,8},{10,9},{11,1... | collective-permute-start | bytes 98312 | tf_op jit(solution)/shard_map/ppermute | solution.py:452
  79.6 6.9 %collective-permute-start.4 = (f32[64,128]{1,0:T(8,128)S(1)}, f32[64,128]{1,0:T(8,128)S(1)}, u32[]{:S(2)}, u32[]{:S(2)}) collective-permute-start(f32[64,128]{1,0:T(8,128)S(1)} %get-tuple-element.16), channel_id=1, source_target_pairs={{0,1},{1,2},{2,3},{3,4},{4,5},{5,6},{6,7},{7,0},{8,9},{9,10},{10,1... | collective-permute-start | bytes 98312 | tf_op jit(solution)/shard_map/ppermute | solution.py:453

commit v5 on v4

--- a/solution.py
+++ b/solution.py
@@ -14,7 +14,7 @@
 SENT = 51
 TILE = 256
 MIB = 1024 * 1024
-HOPS = 3
+HOPS = 2
 
 
 def split(value):
@@ -423,7 +423,7 @@
 
 def wait_for_turn(token):
     count = lax.axis_size("gy")
-    token = token[:1, :CELLS]
+    token = token[0, 0, 0]
     for _ in range(HOPS):
         token = lax.ppermute(
             token, "gy", [(i, (i + 2) % count) for i in range(1, count, 2)]
@@ -437,7 +437,7 @@
     lengths = (rows_y * count_y, rows_z * count_z)
     by_target = spectrum.reshape(6, GROUP, 16, CELLS).transpose(1, 0, 2, 3)
     turn_of = lax.cond(
-        (lax.axis_index("gy") & 1) == 1, wait_for_turn, lambda _: jnp.float32(0.0), offsets
+        (lax.axis_index("gy") & 1) == 1, wait_for_turn, lambda _: jnp.float32(0.0), spectrum
     )
     by_target = jnp.where(turn_of != turn_of, 0.0, by_target)
     received = lax.all_to_all(

time: 88.1 us -> 87.4 us (level); the launches traced: 87.7 us -> 86 us
  waiting for transfers between devices: 9.49 us -> 7.37 us
  starting transfers between devices: 9.59 us -> 7.69 us
  loops' own time: 0.08 us -> 1.27 us
    ppermute x3 -> x2, waiting for transfers between devices: 9.48 us -> 7.37 us  [wait_for_turn(): lax.ppermute(token, 'gy', [(i, (i + 2) % count) for i in range(1, count,...]
    ppermute x3 -> x2, starting transfers between devices: 7.84 us -> 5.93 us  [wait_for_turn(): lax.ppermute(token, 'gy', [(i, (i + 2) % count) for i in range(1, count,...]
    all_to_all x1, blocking collectives: 34.9 us -> 36.7 us  [per_device(): lax.all_to_all(by_target.reshape(GROUP, 96, CELLS), 'gz', split_axis=0, c...]
    all_to_all x1, blocking collectives: 22.1 us -> 20.6 us  [per_device(): owned = lax.all_to_all(lines, 'gz', split_axis=0, concat_axis=0, tiled=True)]
    another operation x1, loops' own time: 0.08 us -> 1.27 us  [per_device(): lax.cond(lax.axis_index('gy') & 1 == 1, wait_for_turn, lambda _: jnp.floa...]
  transfers between devices with their start and end apart: 5 -> 4, of which waited for: 3 -> 2; matrix products, arithmetic and copies ran while one was open for 0% -> 0% of each run, Pallas kernels for 5% -> 5%
where the time goes in v5:
time: 87.4 us; the launch traced here: 86 us
  blocking collectives  57.3 us (66%)
  Pallas kernels  7.74 us (9%)
  starting transfers between devices  7.69 us (9%)
  waiting for transfers between devices  7.37 us (8%)
  local copies, waits for them, and re-layouts  1.65 us (2%)
  other arithmetic  1.52 us (2%)
  between operations  1.41 us (2%)
  loops' own time  1.27 us (1%)
    all_to_all x1, blocking collectives, per_device(): lax.all_to_all(by_target.reshape(GROUP, 96, CELLS), 'gz', split_axis=0, c...  36.7 us
    all_to_all x1, blocking collectives, per_device(): owned = lax.all_to_all(lines, 'gz', split_axis=0, concat_axis=0, tiled=True)  20.6 us
    ppermute x2, waiting for transfers between devices, wait_for_turn(): lax.ppermute(token, 'gy', [(i, (i + 2) % count) for i in range(1, count,...  7.37 us
    ppermute x2, starting transfers between devices, wait_for_turn(): lax.ppermute(token, 'gy', [(i, (i + 2) % count) for i in range(1, count,...  5.93 us
    pallas_call x1, Pallas kernels, interpolate_block(): pl.pallas_call(block_kernel, in_specs=[vmem()] * 3, out_specs=[vmem()] *...  3.47 us
    pallas_call x1, Pallas kernels, transform(): pl.pallas_call(lines_kernel, out_shape=jax.ShapeDtypeStruct((GROUP * SENT...  1.98 us
  transfers between devices with their start and end apart: 4, of which 2 were waited for; matrix products, arithmetic and copies ran while one was open for 0% of the time, Pallas kernels for 5%

profile of v5, /device:TPU:1, one launch (start us, length us, event | category | flops | bytes accessed | tf_op | source)
XLA Modules:
  0.0 86.0 jit_solution(6917331891339054869)
XLA Ops:
  0.6 16.0 %conditional.1 = (pred[]{:T(512)}) conditional(s32[]{:T(128)} %convert_element_type.3, () %tuple.14, f32[3,2,4,128,128]{4,3,2,1,0:T(8,128)} %param.8), branch_computations={%region_0.0_spmd, %region_1.0_spmd} | conditional | flops 1 | bytes 655465 | solution.py:439
  0.6 0.8 slice_bitcast_fusion
  1.5 4.0 %collective-permute-start = (f32[128,128]{1,0:T(8,128)S(1)}, f32[128,128]{1,0:T(8,128)S(1)}, u32[]{:S(2)}, u32[]{:S(2)}) collective-permute-start(f32[128,128]{1,0:T(8,128)S(1)} %slice_bitcast_fusion), channel_id=1, source_target_pairs={{1,3},{3,5},{5,7},{7,1},{9,11},{11,13},{13,15},{15,9},{17,19},{19,... | collective-permute-start | bytes 196616 | tf_op jit(solution)/shard_map/cond/branch_1_fun/ppermute | solution.py:428
  5.5 3.1 %collective-permute-done = f32[128,128]{1,0:T(8,128)S(1)} collective-permute-done((f32[128,128]{1,0:T(8,128)S(1)}, f32[128,128]{1,0:T(8,128)S(1)}, u32[]{:S(2)}, u32[]{:S(2)}) %collective-permute-start) | collective-permute-done | bytes 65568 | tf_op jit(solution)/shard_map/cond/branch_1_fun/ppermute | solution.py:428
  8.6 1.9 %collective-permute-start.1 = (f32[128,128]{1,0:T(8,128)S(1)}, f32[128,128]{1,0:T(8,128)S(1)}, u32[]{:S(2)}, u32[]{:S(2)}) collective-permute-start(f32[128,128]{1,0:T(8,128)S(1)} %collective-permute-done), channel_id=1, source_target_pairs={{1,3},{3,5},{5,7},{7,1},{9,11},{11,13},{13,15},{15,9},{17,19},{19,... | collective-permute-start | bytes 196616 | tf_op jit(solution)/shard_map/cond/branch_1_fun/ppermute | solution.py:428
  10.5 4.3 %collective-permute-done.1 = f32[128,128]{1,0:T(8,128)S(1)} collective-permute-done((f32[128,128]{1,0:T(8,128)S(1)}, f32[128,128]{1,0:T(8,128)S(1)}, u32[]{:S(2)}, u32[]{:S(2)}) %collective-permute-start.1) | collective-permute-done | bytes 65568 | tf_op jit(solution)/shard_map/cond/branch_1_fun/ppermute | solution.py:428
  14.8 0.6 slice.6
  16.6 1.5 %broadcast_select_fusion = f32[3,2,4,128,128]{4,3,2,1,0:T(8,128)S(1)} fusion(f32[3,2,4,128,128]{4,3,2,1,0:T(8,128)} %param.8, pred[]{:T(512)} %get-tuple-element.18), kind=kLoop, calls=%fused_computation.1 | loop fusion | flops 393216 | bytes 3145729 | tf_op jit(solution)/shard_map/jit(_where)/select_n | solution.py:442
  18.2 0.2 copy.10
  18.4 0.0 copy-start
  18.4 0.0 copy-start.1
  18.4 36.7 %all_to_all.10.data = f32[32,96,128]{2,1,0:T(8,128)S(1)} all-to-all(f32[32,96,128]{2,1,0:T(8,128)S(1)} %bitcast.12), channel_id=1, replica_groups=mesh['gz'=32,'gy'=8] {'gz'}, dimensions={0} | all-to-all | bytes 3145728 | tf_op jit(solution)/shard_map/all_to_all | solution.py:443
  55.1 0.0 copy-done
  55.1 0.0 copy-done.1
  55.1 2.0 %lines.1 = f32[1632,128]{1,0:T(8,128)S(1)} custom-call(f32[32,96,128]{2,1,0:T(8,128)S(1)} %all_to_all.10.data, f32[3,32,128]{2,1,0:T(8,128)S(1)} %copy-done.1, bf16[768,128]{1,0:T(8,128)(2,1)S(1)} %copy-done), custom_call_target="tpu_custom_call" | custom-call | tf_op jit(solution)/shard_map/lines/pallas_call | solution.py:176
  57.1 0.0 copy-start.2
  57.1 0.0 copy-start.3
  57.1 20.6 %all_to_all.11 = f32[32,51,1,128]{3,2,1,0:T(1,128)S(1)} all-to-all(f32[32,51,1,128]{3,2,1,0:T(1,128)S(1)} %bitcast.11), channel_id=1, replica_groups=mesh['gz'=32,'gy'=8] {'gz'}, dimensions={0} | all-to-all | bytes 1671168 | tf_op jit(solution)/shard_map/all_to_all | solution.py:447
  77.7 0.0 collective-permute-start.2
  77.8 1.7 %collective-permute-start.3 = (f32[64,128]{1,0:T(8,128)S(1)}, f32[64,128]{1,0:T(8,128)S(1)}, u32[]{:S(2)}, u32[]{:S(2)}) collective-permute-start(f32[64,128]{1,0:T(8,128)S(1)} %get-tuple-element.16), channel_id=1, source_target_pairs={{0,1},{1,2},{2,3},{3,4},{4,5},{5,6},{6,7},{7,0},{8,9},{9,10},{10,1... | collective-permute-start | bytes 98312 | tf_op jit(solution)/shard_map/ppermute | solution.py:453
  80.2 0.0 copy-done.2
  80.2 0.0 copy-done.3
  80.2 1.0 %weights.1 = (bf16[8,512,256]{2,1,0:T(8,128)(2,1)S(1)}, f32[8,152,256]{2,1,0:T(8,128)S(1)}) custom-call(s32[2,2048]{1,0:T(2,128)S(1)} %copy-done.3, f32[3,2048]{1,0:T(4,128)S(1)} %copy-done.2, s32[1]{0:T(128)S(6)} %copy.15.refs_2_), custom_call_target="tpu_custom_call" | custom-call | flops 10000000 | bytes 4000000 | tf_op jit(solution)/shard_map/weights/pallas_call | solution.py:373
  81.2 3.5 %block.1 = (f32[3,4,128,128]{3,2,1,0:T(8,128)}, f32[3,2048]{1,0:T(4,128)S(1)}) custom-call(f32[1632,128]{1,0:T(8,128)S(1)} %bitcast.10, bf16[8,512,256]{2,1,0:T(8,128)(2,1)S(1)} %get-tuple-element.12.near, f32[8,152,256]{2,1,0:T(8,128)S(1)} %get-tuple-element.13.side), custom_call_target="tpu_custom_call" | custom-call | tf_op jit(solution)/shard_map/block/pallas_call | solution.py:392
  84.7 0.0 collective-permute-done.2.above
  84.7 0.0 collective-permute-done.3.below
  84.7 1.3 %edges.1 = f32[3,2048]{1,0:T(4,128)} custom-call(f32[64,128]{1,0:T(8,128)S(1)} %collective-permute-done.2.above, f32[64,128]{1,0:T(8,128)S(1)} %collective-permute-done.3.below, bf16[8,512,256]{2,1,0:T(8,128)(2,1)S(1)} %get-tuple-element.12.near, f32[8,152,256]{2,1,0:T(8,128)S(1)} %get-tuple-element.13.side, f32[3,2048]{1,0:T(4,128)S(1)} %get-tuple-element.17.sums), custom_call_target="tpu_custom_call" | custom-call | tf_op jit(solution)/shard_map/edges/pallas_call | solution.py:410
  (1 shorter events, 0.0 us)
Async XLA Ops:
  1.5 7.1 %collective-permute-start = (f32[128,128]{1,0:T(8,128)S(1)}, f32[128,128]{1,0:T(8,128)S(1)}, u32[]{:S(2)}, u32[]{:S(2)}) collective-permute-start(f32[128,128]{1,0:T(8,128)S(1)} %slice_bitcast_fusion), channel_id=1, source_target_pairs={{1,3},{3,5},{5,7},{7,1},{9,11},{11,13},{13,15},{15,9},{17,19},{19,... | collective-permute-start | bytes 196616 | tf_op jit(solution)/shard_map/cond/branch_1_fun/ppermute | solution.py:428
  8.6 6.2 %collective-permute-start.1 = (f32[128,128]{1,0:T(8,128)S(1)}, f32[128,128]{1,0:T(8,128)S(1)}, u32[]{:S(2)}, u32[]{:S(2)}) collective-permute-start(f32[128,128]{1,0:T(8,128)S(1)} %collective-permute-done), channel_id=1, source_target_pairs={{1,3},{3,5},{5,7},{7,1},{9,11},{11,13},{13,15},{15,9},{17,19},{19,... | collective-permute-start | bytes 196616 | tf_op jit(solution)/shard_map/cond/branch_1_fun/ppermute | solution.py:428
  18.4 36.7 %copy-start = (bf16[768,128]{1,0:T(8,128)(2,1)S(1)}, bf16[768,128]{1,0:T(8,128)(2,1)}, u32[]{:S(2)}) copy-start(bf16[768,128]{1,0:T(8,128)(2,1)} %constant.15.clone.matrix) | copy-start | bytes 589828
  18.4 36.7 %copy-start.1 = (f32[3,32,128]{2,1,0:T(8,128)S(1)}, f32[3,32,128]{2,1,0:T(8,128)}, u32[]{:S(2)}) copy-start(f32[3,32,128]{2,1,0:T(8,128)} %constant.14.clone.table) | copy-start | bytes 147460
  57.1 23.1 %copy-start.2 = (f32[3,2048]{1,0:T(4,128)S(1)}, f32[3,2048]{1,0:T(4,128)}, u32[]{:S(2)}) copy-start(f32[3,2048]{1,0:T(4,128)} %refs_1_.1) | copy-start | bytes 73732
  57.1 23.1 %copy-start.3 = (s32[2,2048]{1,0:T(2,128)S(1)}, s32[2,2048]{1,0:T(2,128)}, u32[]{:S(2)}) copy-start(s32[2,2048]{1,0:T(2,128)} %refs_0_.1) | copy-start | bytes 49156
  77.7 6.9 %collective-permute-start.2 = (f32[64,128]{1,0:T(8,128)S(1)}, f32[64,128]{1,0:T(8,128)S(1)}, u32[]{:S(2)}, u32[]{:S(2)}) collective-permute-start(f32[64,128]{1,0:T(8,128)S(1)} %get-tuple-element.15), channel_id=1, source_target_pairs={{1,0},{2,1},{3,2},{4,3},{5,4},{6,5},{7,6},{0,7},{9,8},{10,9},{11,1... | collective-permute-start | bytes 98312 | tf_op jit(solution)/shard_map/ppermute | solution.py:452
  77.8 6.9 %collective-permute-start.3 = (f32[64,128]{1,0:T(8,128)S(1)}, f32[64,128]{1,0:T(8,128)S(1)}, u32[]{:S(2)}, u32[]{:S(2)}) collective-permute-start(f32[64,128]{1,0:T(8,128)S(1)} %get-tuple-element.16), channel_id=1, source_target_pairs={{0,1},{1,2},{2,3},{3,4},{4,5},{5,6},{6,7},{7,0},{8,9},{9,10},{10,1... | collective-permute-start | bytes 98312 | tf_op jit(solution)/shard_map/ppermute | solution.py:453

commit v6 on v5

--- a/solution.py
+++ b/solution.py
@@ -423,7 +423,7 @@
 
 def wait_for_turn(token):
     count = lax.axis_size("gy")
-    token = token[0, 0, 0]
+    token = token[0, 0, 0, :96]
     for _ in range(HOPS):
         token = lax.ppermute(
             token, "gy", [(i, (i + 2) % count) for i in range(1, count, 2)]

time: 87.4 us -> 87.8 us (level)
  the two profiles are of different devices: /device:TPU:1 before, /device:TPU:25 now
where the time goes in v6:
time: 87.8 us; the launch traced here: 87.4 us
  blocking collectives  61.3 us (70%)
  starting transfers between devices  7.99 us (9%)
  Pallas kernels  7.73 us (9%)
  waiting for transfers between devices  4.61 us (5%)
  local copies, waits for them, and re-layouts  1.6 us (2%)
  other arithmetic  1.52 us (2%)
  between operations  1.41 us (2%)
  loops' own time  1.27 us (1%)
    all_to_all x1, blocking collectives, per_device(): lax.all_to_all(by_target.reshape(GROUP, 96, CELLS), 'gz', split_axis=0, c...  39.6 us
    all_to_all x1, blocking collectives, per_device(): owned = lax.all_to_all(lines, 'gz', split_axis=0, concat_axis=0, tiled=True)  21.7 us
    ppermute x2, starting transfers between devices, wait_for_turn(): lax.ppermute(token, 'gy', [(i, (i + 2) % count) for i in range(1, count,...  5.03 us
    ppermute x2, waiting for transfers between devices, wait_for_turn(): lax.ppermute(token, 'gy', [(i, (i + 2) % count) for i in range(1, count,...  4.6 us
    pallas_call x1, Pallas kernels, interpolate_block(): pl.pallas_call(block_kernel, in_specs=[vmem()] * 3, out_specs=[vmem()] *...  3.46 us
    ppermute x1, starting transfers between devices, per_device(): below = lax.ppermute(top, 'gy', forward)  2.94 us
    pallas_call x1, Pallas kernels, transform(): pl.pallas_call(lines_kernel, out_shape=jax.ShapeDtypeStruct((GROUP * SENT...  1.98 us
  transfers between devices with their start and end apart: 4, of which 2 were waited for; matrix products, arithmetic and copies ran while one was open for 0% of the time, Pallas kernels for 5%

profile of v6, /device:TPU:25, one launch (start us, length us, event | category | flops | bytes accessed | tf_op | source)
XLA Modules:
  0.0 87.4 jit_solution(17273400157596089968)
XLA Ops:
  0.6 12.3 %conditional.1 = (pred[]{:T(512)}) conditional(s32[]{:T(128)} %convert_element_type.3, () %tuple.14, f32[3,2,4,128,128]{4,3,2,1,0:T(8,128)} %param.8), branch_computations={%region_0.0_spmd, %region_1.0_spmd} | conditional | flops 1 | bytes 491625 | solution.py:439
  0.6 0.8 slice_bitcast_fusion
  1.5 1.9 %collective-permute-start = (f32[96,128]{1,0:T(8,128)S(1)}, f32[96,128]{1,0:T(8,128)S(1)}, u32[]{:S(2)}, u32[]{:S(2)}) collective-permute-start(f32[96,128]{1,0:T(8,128)S(1)} %slice_bitcast_fusion), channel_id=1, source_target_pairs={{1,3},{3,5},{5,7},{7,1},{9,11},{11,13},{13,15},{15,9},{17,19},{19,... | collective-permute-start | bytes 147464 | tf_op jit(solution)/shard_map/cond/branch_1_fun/ppermute | solution.py:428
  3.4 2.9 %collective-permute-done = f32[96,128]{1,0:T(8,128)S(1)} collective-permute-done((f32[96,128]{1,0:T(8,128)S(1)}, f32[96,128]{1,0:T(8,128)S(1)}, u32[]{:S(2)}, u32[]{:S(2)}) %collective-permute-start) | collective-permute-done | bytes 49184 | tf_op jit(solution)/shard_map/cond/branch_1_fun/ppermute | solution.py:428
  6.3 3.1 %collective-permute-start.1 = (f32[96,128]{1,0:T(8,128)S(1)}, f32[96,128]{1,0:T(8,128)S(1)}, u32[]{:S(2)}, u32[]{:S(2)}) collective-permute-start(f32[96,128]{1,0:T(8,128)S(1)} %collective-permute-done), channel_id=1, source_target_pairs={{1,3},{3,5},{5,7},{7,1},{9,11},{11,13},{13,15},{15,9},{17,19},{19,... | collective-permute-start | bytes 147464 | tf_op jit(solution)/shard_map/cond/branch_1_fun/ppermute | solution.py:428
  9.4 1.7 %collective-permute-done.1 = f32[96,128]{1,0:T(8,128)S(1)} collective-permute-done((f32[96,128]{1,0:T(8,128)S(1)}, f32[96,128]{1,0:T(8,128)S(1)}, u32[]{:S(2)}, u32[]{:S(2)}) %collective-permute-start.1) | collective-permute-done | bytes 49184 | tf_op jit(solution)/shard_map/cond/branch_1_fun/ppermute | solution.py:428
  11.1 0.6 slice.6
  12.9 1.5 %broadcast_select_fusion = f32[3,2,4,128,128]{4,3,2,1,0:T(8,128)S(1)} fusion(f32[3,2,4,128,128]{4,3,2,1,0:T(8,128)} %param.8, pred[]{:T(512)} %get-tuple-element.18), kind=kLoop, calls=%fused_computation.1 | loop fusion | flops 393216 | bytes 3145729 | tf_op jit(solution)/shard_map/jit(_where)/select_n | solution.py:442
  14.5 0.2 copy.10
  14.7 0.0 copy-start
  14.7 0.0 copy-start.1
  14.7 39.6 %all_to_all.10.data = f32[32,96,128]{2,1,0:T(8,128)S(1)} all-to-all(f32[32,96,128]{2,1,0:T(8,128)S(1)} %bitcast.12), channel_id=1, replica_groups=mesh['gz'=32,'gy'=8] {'gz'}, dimensions={0} | all-to-all | bytes 3145728 | tf_op jit(solution)/shard_map/all_to_all | solution.py:443
  54.2 0.0 copy-done
  54.2 0.0 copy-done.1
  54.2 2.0 %lines.1 = f32[1632,128]{1,0:T(8,128)S(1)} custom-call(f32[32,96,128]{2,1,0:T(8,128)S(1)} %all_to_all.10.data, f32[3,32,128]{2,1,0:T(8,128)S(1)} %copy-done.1, bf16[768,128]{1,0:T(8,128)(2,1)S(1)} %copy-done), custom_call_target="tpu_custom_call" | custom-call | tf_op jit(solution)/shard_map/lines/pallas_call | solution.py:176
  56.2 0.0 copy-start.2
  56.3 0.0 copy-start.3
  56.3 21.7 %all_to_all.11 = f32[32,51,1,128]{3,2,1,0:T(1,128)S(1)} all-to-all(f32[32,51,1,128]{3,2,1,0:T(1,128)S(1)} %bitcast.11), channel_id=1, replica_groups=mesh['gz'=32,'gy'=8] {'gz'}, dimensions={0} | all-to-all | bytes 1671168 | tf_op jit(solution)/shard_map/all_to_all | solution.py:447
  78.0 0.0 collective-permute-start.2
  78.0 2.9 %collective-permute-start.3 = (f32[64,128]{1,0:T(8,128)S(1)}, f32[64,128]{1,0:T(8,128)S(1)}, u32[]{:S(2)}, u32[]{:S(2)}) collective-permute-start(f32[64,128]{1,0:T(8,128)S(1)} %get-tuple-element.16), channel_id=1, source_target_pairs={{0,1},{1,2},{2,3},{3,4},{4,5},{5,6},{6,7},{7,0},{8,9},{9,10},{10,1... | collective-permute-start | bytes 98312 | tf_op jit(solution)/shard_map/ppermute | solution.py:453
  81.6 0.0 copy-done.2
  81.6 0.0 copy-done.3
  81.7 1.0 %weights.1 = (bf16[8,512,256]{2,1,0:T(8,128)(2,1)S(1)}, f32[8,152,256]{2,1,0:T(8,128)S(1)}) custom-call(s32[2,2048]{1,0:T(2,128)S(1)} %copy-done.3, f32[3,2048]{1,0:T(4,128)S(1)} %copy-done.2, s32[1]{0:T(128)S(6)} %copy.15.refs_2_), custom_call_target="tpu_custom_call" | custom-call | flops 10000000 | bytes 4000000 | tf_op jit(solution)/shard_map/weights/pallas_call | solution.py:373
  82.7 3.5 %block.1 = (f32[3,4,128,128]{3,2,1,0:T(8,128)}, f32[3,2048]{1,0:T(4,128)S(1)}) custom-call(f32[1632,128]{1,0:T(8,128)S(1)} %bitcast.10, bf16[8,512,256]{2,1,0:T(8,128)(2,1)S(1)} %get-tuple-element.12.near, f32[8,152,256]{2,1,0:T(8,128)S(1)} %get-tuple-element.13.side), custom_call_target="tpu_custom_call" | custom-call | tf_op jit(solution)/shard_map/block/pallas_call | solution.py:392
  86.2 0.0 collective-permute-done.2.above
  86.2 0.0 collective-permute-done.3.below
  86.2 1.2 %edges.1 = f32[3,2048]{1,0:T(4,128)} custom-call(f32[64,128]{1,0:T(8,128)S(1)} %collective-permute-done.2.above, f32[64,128]{1,0:T(8,128)S(1)} %collective-permute-done.3.below, bf16[8,512,256]{2,1,0:T(8,128)(2,1)S(1)} %get-tuple-element.12.near, f32[8,152,256]{2,1,0:T(8,128)S(1)} %get-tuple-element.13.side, f32[3,2048]{1,0:T(4,128)S(1)} %get-tuple-element.17.sums), custom_call_target="tpu_custom_call" | custom-call | tf_op jit(solution)/shard_map/edges/pallas_call | solution.py:410
  (1 shorter events, 0.0 us)
Async XLA Ops:
  1.5 4.8 %collective-permute-start = (f32[96,128]{1,0:T(8,128)S(1)}, f32[96,128]{1,0:T(8,128)S(1)}, u32[]{:S(2)}, u32[]{:S(2)}) collective-permute-start(f32[96,128]{1,0:T(8,128)S(1)} %slice_bitcast_fusion), channel_id=1, source_target_pairs={{1,3},{3,5},{5,7},{7,1},{9,11},{11,13},{13,15},{15,9},{17,19},{19,... | collective-permute-start | bytes 147464 | tf_op jit(solution)/shard_map/cond/branch_1_fun/ppermute | solution.py:428
  6.3 4.8 %collective-permute-start.1 = (f32[96,128]{1,0:T(8,128)S(1)}, f32[96,128]{1,0:T(8,128)S(1)}, u32[]{:S(2)}, u32[]{:S(2)}) collective-permute-start(f32[96,128]{1,0:T(8,128)S(1)} %collective-permute-done), channel_id=1, source_target_pairs={{1,3},{3,5},{5,7},{7,1},{9,11},{11,13},{13,15},{15,9},{17,19},{19,... | collective-permute-start | bytes 147464 | tf_op jit(solution)/shard_map/cond/branch_1_fun/ppermute | solution.py:428
  14.7 39.6 %copy-start = (bf16[768,128]{1,0:T(8,128)(2,1)S(1)}, bf16[768,128]{1,0:T(8,128)(2,1)}, u32[]{:S(2)}) copy-start(bf16[768,128]{1,0:T(8,128)(2,1)} %constant.15.clone.matrix) | copy-start | bytes 589828
  14.7 39.6 %copy-start.1 = (f32[3,32,128]{2,1,0:T(8,128)S(1)}, f32[3,32,128]{2,1,0:T(8,128)}, u32[]{:S(2)}) copy-start(f32[3,32,128]{2,1,0:T(8,128)} %constant.14.clone.table) | copy-start | bytes 147460
  56.2 25.4 %copy-start.2 = (f32[3,2048]{1,0:T(4,128)S(1)}, f32[3,2048]{1,0:T(4,128)}, u32[]{:S(2)}) copy-start(f32[3,2048]{1,0:T(4,128)} %refs_1_.1) | copy-start | bytes 73732
  56.3 25.4 %copy-start.3 = (s32[2,2048]{1,0:T(2,128)S(1)}, s32[2,2048]{1,0:T(2,128)}, u32[]{:S(2)}) copy-start(s32[2,2048]{1,0:T(2,128)} %refs_0_.1) | copy-start | bytes 49156
  78.0 8.1 %collective-permute-start.2 = (f32[64,128]{1,0:T(8,128)S(1)}, f32[64,128]{1,0:T(8,128)S(1)}, u32[]{:S(2)}, u32[]{:S(2)}) collective-permute-start(f32[64,128]{1,0:T(8,128)S(1)} %get-tuple-element.15), channel_id=1, source_target_pairs={{1,0},{2,1},{3,2},{4,3},{5,4},{6,5},{7,6},{0,7},{9,8},{10,9},{11,1... | collective-permute-start | bytes 98312 | tf_op jit(solution)/shard_map/ppermute | solution.py:452
  78.0 8.1 %collective-permute-start.3 = (f32[64,128]{1,0:T(8,128)S(1)}, f32[64,128]{1,0:T(8,128)S(1)}, u32[]{:S(2)}, u32[]{:S(2)}) collective-permute-start(f32[64,128]{1,0:T(8,128)S(1)} %get-tuple-element.16), channel_id=1, source_target_pairs={{0,1},{1,2},{2,3},{3,4},{4,5},{5,6},{6,7},{7,0},{8,9},{9,10},{10,1... | collective-permute-start | bytes 98312 | tf_op jit(solution)/shard_map/ppermute | solution.py:453
